TPU v7x, 256 devices: a whole 4x4x8 slice. The times are simulated.
256 devices in a mesh: comp: 16 (over y, z_lo, core), space: 16 (over x, z_hi).
Axes of the slice: x: 4, y: 4, z: 8 (z_hi: 4, z_lo: 2; z = z_hi * 2 + z_lo), core: 2. Of those that a mesh axis runs over, the one named last changes fastest.
Arguments:
- adjoint_forcing: float32 [384, 512, 1024], P('comp', 'space'), may hold values from -6 to 6
- forward_state: bfloat16 [384, 512, 1024], P(None, ('space', 'comp')), may hold values from -6 to 6
- wind_speed: float32 [512, 1024], P(('space', 'comp')), may hold values from 0.5 to 2
- cg_index: int32 [16, 512, 1024], P('comp', 'space'), may hold values from 0 to 7
- turn_index: int32 [16, 512, 1024], P('comp', 'space'), may hold values from 0 to 7
- sea_mask: int32 [512, 1024], P('space'), may hold values 0 or 1
- dir_sign: int32 [2, 24], replicated, may hold values from -1 to 1, as said below
- w_in: bfloat16 [1536, 384], replicated, may hold values from -0.3125 to 0.3125
- w_out: bfloat16 [384, 1536], replicated, may hold values from -0.15625 to 0.15625
- wind_weight: float32 [1536], replicated, may hold values from -6 to 6
Outputs:
- adjoint_start: float32 [384, 512, 1024], P('comp', 'space')
- wind_gradient: float32 [512, 1024], P(('space', 'comp'))
Inputs may be any that keep to these rules, and one draw needn't show every extreme that they name: `dir_sign`: every entry is -1 or 1.
All inputs are finite; a program needn't handle non-finite values. No bound on the sum of `sea_mask` on one device may be relied on, other than what follows from the above.
Results may differ from a plain program's by a relative error of at most 0.0035.
Values may be sent and summed in bfloat16 or wider, within the bound.
A program may use at most 64 MiB of HBM per device.

v0:
```python
import math

import jax
import jax.numpy as jnp
from jax import lax
from jax.sharding import PartitionSpec as P

STEPS = 2


def extended(block, sides, width):
    for axis, dim in sides:
        count = lax.axis_size(axis)
        forward = [(i, i + 1) for i in range(count - 1)]
        backward = [(target, source) for source, target in forward]
        low = lax.ppermute(
            lax.slice_in_dim(block, block.shape[dim] - width, None, axis=dim), axis, forward
        )
        high = lax.ppermute(lax.slice_in_dim(block, 0, width, axis=dim), axis, backward)
        block = jnp.concatenate([low, block, high], axis=dim)
    return block


def direction_factors(dirs):
    angle = (jnp.arange(dirs, dtype=jnp.float32) + 0.5) * (2.0 * math.pi / dirs)
    return (0.5 * jnp.abs(jnp.cos(angle)), 0.5 * jnp.abs(jnp.sin(angle)))


def adjoint_step(costate, celerity, turning, turn_up, sea_land, sign_x, sign_y, along_x, along_y):
    cour_x = along_x * celerity
    cour_y = along_y * celerity
    masked = costate * sea_land
    retained = (1.0 - cour_x - cour_y - turning) * masked
    flux_x = cour_x * masked
    flux_y = cour_y * masked
    flux_t = turning * masked
    zero_col = jnp.zeros_like(flux_x[..., :1])
    from_right = jnp.concatenate([flux_x[..., 1:], zero_col], axis=-1)
    from_left = jnp.concatenate([zero_col, flux_x[..., :-1]], axis=-1)
    term_x = jnp.where(sign_x > 0, from_right, from_left)
    padded = extended(flux_y, (("space", 2),), 1)
    term_y = jnp.where(sign_y > 0, padded[:, :, 2:, :], padded[:, :, :-2, :])
    term_t = jnp.where(turn_up, jnp.roll(flux_t, -1, axis=-3), jnp.roll(flux_t, 1, axis=-3))
    return retained + term_x + term_y + term_t


def source_adjoint(cell_half, cell_state, cell_wind, w_in, w_out, wind_weight):
    pulled = lax.dot_general(
        w_out, cell_half, (((0,), (0,)), ((), ())), preferred_element_type=jnp.float32
    )
    forward = (
        jnp.dot(w_in, cell_state, preferred_element_type=jnp.float32)
        + wind_weight[:, None] * cell_wind[None, :]
    )
    squash = jnp.tanh(forward)
    weighted = (1.0 - squash * squash) * pulled
    increment = lax.dot_general(
        w_in,
        weighted.astype(jnp.bfloat16),
        (((0,), (0,)), ((), ())),
        preferred_element_type=jnp.float32,
    ).astype(jnp.bfloat16)
    wind_grad = jnp.sum(wind_weight[:, None] * weighted, axis=0)
    return (increment, wind_grad)


def shards(
    adjoint_forcing,
    forward_state,
    wind_speed,
    cg_index,
    turn_index,
    sea_mask,
    dir_sign,
    w_in,
    w_out,
    wind_weight,
):
    dirs = dir_sign.shape[1]
    comps, rows, cols = adjoint_forcing.shape
    freqs = comps // dirs
    total_comps = w_in.shape[1]
    along_x, along_y = direction_factors(dirs)
    along_x = along_x.reshape(1, dirs, 1, 1)
    along_y = along_y.reshape(1, dirs, 1, 1)
    sign_x = dir_sign[0].reshape(1, dirs, 1, 1)
    sign_y = dir_sign[1].reshape(1, dirs, 1, 1)
    sea_land = sea_mask.astype(jnp.float32)
    celerity = (0.1 + 0.8 * cg_index.astype(jnp.float32) / 7.0)[:, None]
    turning = (0.3 * jnp.abs(turn_index.astype(jnp.float32) - 3.5) / 3.5)[:, None]
    turn_up = (turn_index >= 4)[:, None]
    costate = adjoint_forcing.reshape(freqs, dirs, rows, cols)
    for sweep in range(STEPS):
        costate = adjoint_step(
            costate, celerity, turning, turn_up, sea_land, sign_x, sign_y, along_x, along_y
        )
    costate = costate.reshape(comps, rows, cols)
    cell_state = forward_state.reshape(total_comps, -1)
    cell_wind = wind_speed.reshape(-1)
    cell_costate = lax.all_to_all(costate, "comp", split_axis=1, concat_axis=0, tiled=True)
    increment, wind_grad = source_adjoint(
        cell_costate.reshape(total_comps, -1).astype(jnp.bfloat16),
        cell_state,
        cell_wind,
        w_in,
        w_out,
        wind_weight,
    )
    cell_start = cell_costate + increment.astype(jnp.float32).reshape(cell_costate.shape)
    adjoint_start = lax.all_to_all(cell_start, "comp", split_axis=0, concat_axis=1, tiled=True)
    return (adjoint_start, wind_grad.reshape(wind_speed.shape))


def solution(mesh):
    placed = (
        P("comp", "space", None),
        P(None, ("space", "comp"), None),
        P(("space", "comp"), None),
        P("comp", "space", None),
        P("comp", "space", None),
        P("space", None),
        P(),
        P(),
        P(),
        P(),
    )
    return jax.shard_map(
        shards,
        mesh=mesh,
        in_specs=placed,
        out_specs=(P("comp", "space", None), P(("space", "comp"), None)),
        check_vma=False,
    )
```

profile of v0, /device:TPU:7, one launch (start us, length us, event | category | flops | bytes accessed | tf_op | source)
XLA Modules:
  0.0 184.7 jit_solution(16925243396143729044)
XLA Ops:
  0.6 0.0 copy-start
  0.7 1.0 convert_element_type.28
  1.7 1.0 multiply_bitcast_fusion.1
  2.7 4.3 %fusion.8 = (f32[1,24,32,1024]{3,1,2,0:T(8,128)S(1)}, f32[1,24,32,1024]{3,1,2,0:T(8,128)S(1)}, f32[1,24,32,1024]{3,1,2,0:T(8,128)S(1)}) fusion(f32[24,32,1024]{2,1,0:T(8,128)} %param.10, f32[32,1024]{1,0:T(8,128)S(1)} %convert_element_type.28, f32[32,1024]{1,0:T(8,128)S(1)} %get-tuple-element.34, f32[24]{0:T(128)S(1)} %get-tuple-element.36, ...), kind=kLoop, calls=%fused_computation.18 | loop fusion | flops 4718592 | bytes 12976320 | tf_op jit(solution)/shard_map/mul | solution.py:34
  7.0 8.2 %collective-permute-start = (f32[1,24,1,1024]{3,1,2,0:T(8,128)S(1)}, f32[1,24,1,1024]{3,1,2,0:T(8,128)S(1)}, u32[]{:S(2)}, u32[]{:S(2)}) collective-permute-start(f32[1,24,1,1024]{3,1,2,0:T(8,128)S(1)} %get-tuple-element.23), channel_id=1, source_target_pairs={{1,0},{2,1},{3,2},{4,3},{5,4},{6,5},{7,6},{8,7},{9,8},{10,9},{11,1... | collective-permute-start | bytes 294920 | tf_op jit(solution)/shard_map/ppermute | solution.py:19
  15.2 1.9 %collective-permute-start.1 = (f32[1,24,1,1024]{3,1,2,0:T(8,128)S(1)}, f32[1,24,1,1024]{3,1,2,0:T(8,128)S(1)}, u32[]{:S(2)}, u32[]{:S(2)}) collective-permute-start(f32[1,24,1,1024]{3,1,2,0:T(8,128)S(1)} %get-tuple-element.24), channel_id=1, source_target_pairs={{0,1},{1,2},{2,3},{3,4},{4,5},{5,6},{6,7},{7,8},{8,9},{9,10},{10,1... | collective-permute-start | bytes 294920 | tf_op jit(solution)/shard_map/ppermute | solution.py:16
  17.2 0.0 copy-start.5
  17.2 0.7 fusion.32
  17.9 0.2 fusion.33
  18.2 0.0 copy-done.5
  18.2 0.0 copy-start.7
  18.2 0.0 copy-start.1
  18.2 3.8 %fusion.30 = (f32[1,24,32,1023]{3,1,2,0:T(8,128)}, f32[1,24,32,1023]{3,1,2,0:T(8,128)}) fusion(f32[1,24,32,1024]{3,1,2,0:T(8,128)S(1)} %get-tuple-element.8), kind=kLoop, calls=%fused_computation.54 | loop fusion | bytes 12570624 | tf_op jit(solution)/shard_map/slice | solution.py:38
  22.0 0.0 copy-done.7
  22.0 0.0 collective-permute-done
  22.0 2.7 %collective-permute-done.1 = f32[1,24,1,1024]{3,1,2,0:T(8,128)S(1)} collective-permute-done((f32[1,24,1,1024]{3,1,2,0:T(8,128)S(1)}, f32[1,24,1,1024]{3,1,2,0:T(8,128)S(1)}, u32[]{:S(2)}, u32[]{:S(2)}) %collective-permute-start.1) | collective-permute-done | bytes 98336 | tf_op jit(solution)/shard_map/ppermute | solution.py:16
  24.7 0.0 copy-done.1
  24.8 9.3 %multiply_multiply_fusion.3 = (f32[1,24,32,1024]{3,1,2,0:T(8,128)S(1)}, f32[1,24,32,1024]{3,1,2,0:T(8,128)S(1)}) fusion(f32[32,1024]{1,0:T(8,128)S(1)} %get-tuple-element.34, f32[24]{0:T(128)S(1)} %get-tuple-element.36, f32[32,1024]{1,0:T(8,128)S(1)} %convert_element_type.28, f32[1,23,32,1024]{3,1,2,0:T(8,128)S(1)} %get-tuple-element.26, ...), kind=kLoop, calls=%fused_computation.10 | loop fusion | flops 15728640 | bytes 25782512 | tf_op jit(solution)/shard_map/mul | solution.py:34
  34.1 0.6 broadcast_multiply_fusion
  34.7 0.7 fusion.28
  35.4 3.7 %collective-permute-start.2 = (f32[1,24,1,1024]{3,1,2,0:T(8,128)S(1)}, f32[1,24,1,1024]{3,1,2,0:T(8,128)S(1)}, u32[]{:S(2)}, u32[]{:S(2)}) collective-permute-start(f32[1,24,1,1024]{3,1,2,0:T(8,128)S(1)} %get-tuple-element.19), channel_id=1, source_target_pairs={{1,0},{2,1},{3,2},{4,3},{5,4},{6,5},{7,6},{8,7},{9,8},{10,9},{11,1... | collective-permute-start | bytes 294920 | tf_op jit(solution)/shard_map/ppermute | solution.py:19
  39.1 2.7 %collective-permute-start.3 = (f32[1,24,1,1024]{3,1,2,0:T(8,128)S(1)}, f32[1,24,1,1024]{3,1,2,0:T(8,128)S(1)}, u32[]{:S(2)}, u32[]{:S(2)}) collective-permute-start(f32[1,24,1,1024]{3,1,2,0:T(8,128)S(1)} %get-tuple-element.20), channel_id=1, source_target_pairs={{0,1},{1,2},{2,3},{3,4},{4,5},{5,6},{6,7},{7,8},{8,9},{9,10},{10,1... | collective-permute-start | bytes 294920 | tf_op jit(solution)/shard_map/ppermute | solution.py:16
  41.8 1.3 fusion.26
  43.0 0.2 fusion.27
  43.3 0.0 collective-permute-done.2
  43.3 5.9 %collective-permute-done.3 = f32[1,24,1,1024]{3,1,2,0:T(8,128)S(1)} collective-permute-done((f32[1,24,1,1024]{3,1,2,0:T(8,128)S(1)}, f32[1,24,1,1024]{3,1,2,0:T(8,128)S(1)}, u32[]{:S(2)}, u32[]{:S(2)}) %collective-permute-start.3) | collective-permute-done | bytes 98336 | tf_op jit(solution)/shard_map/ppermute | solution.py:16
  49.2 5.3 %fusion.7 = f32[24,32,1024]{2,0,1:T(8,128)} fusion(f32[1,24,32,1024]{3,1,2,0:T(8,128)S(1)} %get-tuple-element.7, f32[1,24,32,1024]{3,1,2,0:T(8,128)S(1)} %get-tuple-element.18, f32[1,24,1,1024]{3,1,2,0:T(8,128)S(1)} %collective-permute-done.3, f32[1,24,1,1024]{3,1,2,0:T(8,128)S(1)} %collective-permute-done.2, f32[1,1,32,1024]{3,1,2,0:T(1,128)S(1)} %get-tuple-element.14, ...), kind=kLoop, calls=%fused_computation.17 | loop fusion | flops 12582912 | bytes 22505712 | tf_op jit(solution)/shard_map/reshape | solution.py:97
  54.4 0.0 copy-start.2
  54.5 7.6 %all-to-all-start = ((f32[24,32,1024]{2,0,1:T(8,128)}), f32[24,32,1024]{2,0,1:T(8,128)}, u32[]{:S(2)}, u32[]{:S(2)}) async-start(f32[24,32,1024]{2,0,1:T(8,128)} %fusion.7), calls=%async_computation | async-start | bytes 6291456 | tf_op jit(solution)/shard_map/all_to_all | solution.py:100
  62.1 0.0 copy-start.6
  62.1 0.0 copy-done.2
  62.1 1.6 copy.30
  63.7 0.0 copy-done.6
  63.7 36.8 %all-to-all-done = f32[24,32,1024]{2,0,1:T(8,128)} async-done(((f32[24,32,1024]{2,0,1:T(8,128)}), f32[24,32,1024]{2,0,1:T(8,128)}, u32[]{:S(2)}, u32[]{:S(2)}) %all-to-all-start) | async-done | bytes 3145760 | tf_op jit(solution)/shard_map/all_to_all | solution.py:100
  100.5 2.1 %convert_element_type.29 = bf16[16,24,2,1024]{3,1,2,0:T(8,128)(2,1)S(1)} convert(f32[16,24,2,1024]{3,1,2,0:T(8,128)} %bitcast.11) | non-fusion elementwise | flops 786432 | bytes 4718592 | tf_op jit(solution)/shard_map/convert_element_type | solution.py:102
  102.7 3.9 %copy.23 = f32[16,24,2,1024]{3,1,0,2:T(8,128)} copy(f32[16,24,2,1024]{3,1,2,0:T(8,128)} %bitcast.11) | data formatting | bytes 6291456 | tf_op jit(solution)/shard_map/all_to_all | solution.py:100
  106.6 0.0 copy-start.4
  106.6 1.6 copy.24
  108.2 0.4 copy.32
  108.7 0.0 copy-done.4
  108.7 0.0 copy-start.3
  108.7 0.0 copy-start.8
  108.7 3.5 %fusion.34 = f32[2048,1536]{0,1:T(8,128)S(1)} fusion(bf16[384,2048]{1,0:T(8,128)(2,1)S(1)} %bitcast.60, bf16[384,1536]{1,0:T(8,128)(2,1)S(1)} %copy-done.4), kind=kOutput, calls=%fused_computation.58 | convolution fusion | flops 2415919104 | bytes 15335424 | tf_op jit(solution)/shard_map/dot_general | solution.py:48
  112.2 0.0 copy-done
  112.2 0.0 copy-done.3
  112.2 0.0 copy-done.8
  112.2 5.6 %multiply_reduce_fusion = (f32[2048]{0:T(1024)S(1)}, bf16[1536,2048]{1,0:T(8,128)(2,1)S(1)}) fusion(f32[1536]{0:T(1024)S(1)} %copy-done.8, f32[2048,1536]{0,1:T(8,128)S(1)} %fusion.34, f32[2048]{0:T(1024)S(1)} %bitcast.66, bf16[1536,384]{1,0:T(8,128)(2,1)S(1)} %copy-done, bf16[384,2048]{1,0:T(8,128)(2,1)S(1)} %bitcast.64), kind=kOutput, calls=%fused_computation.1 | convolution fusion | flops 2441082880 | bytes 21649408 | tf_op jit(solution)/shard_map/dot_general | solution.py:52
  117.8 5.2 %fusion.22 = f32[2048,384]{1,0:T(8,128)} fusion(bf16[1536,384]{1,0:T(8,128)(2,1)S(1)} %copy-done, bf16[1536,2048]{1,0:T(8,128)(2,1)S(1)} %get-tuple-element.32), kind=kOutput, calls=%fused_computation.39 | convolution fusion | flops 2417491968 | bytes 10616832 | tf_op jit(solution)/shard_map/dot_general | solution.py:57
  123.1 3.6 %copy.25 = f32[384,2,1024]{2,0,1:T(8,128)} copy(f32[384,2,1024]{0,2,1:T(8,128)} %bitcast.62) | data formatting | bytes 6291456 | tf_op jit(solution)/shard_map/reshape | solution.py:109
  126.7 3.5 %bitcast_add_fusion = f32[384,2,1024]{2,0,1:T(8,128)S(1)} fusion(f32[384,2,1024]{2,0,1:T(8,128)} %copy.25, f32[16,24,2,1024]{3,1,0,2:T(8,128)} %copy.23), kind=kLoop, calls=%fused_computation.35 | loop fusion | flops 786432 | bytes 9437184 | tf_op jit(solution)/shard_map/add | solution.py:109
  130.2 4.1 %copy.26 = f32[384,2,1024]{2,1,0:T(2,128)} copy(f32[384,2,1024]{2,0,1:T(8,128)S(1)} %bitcast_add_fusion) | data formatting | bytes 6291456 | tf_op jit(solution)/shard_map/add | solution.py:109
  134.3 5.1 %all-to-all-start.1 = ((f32[384,2,1024]{2,1,0:T(2,128)}), f32[384,2,1024]{2,1,0:T(2,128)}, u32[]{:S(2)}, u32[]{:S(2)}) async-start(f32[384,2,1024]{2,1,0:T(2,128)} %copy.26), calls=%async_computation.1 | async-start | bytes 6291456 | tf_op jit(solution)/shard_map/all_to_all | solution.py:110
  139.3 0.6 reshape.211
  140.0 37.9 %all-to-all-done.1 = f32[384,2,1024]{2,1,0:T(2,128)} async-done(((f32[384,2,1024]{2,1,0:T(2,128)}), f32[384,2,1024]{2,1,0:T(2,128)}, u32[]{:S(2)}, u32[]{:S(2)}) %all-to-all-start.1) | async-done | bytes 3145760 | tf_op jit(solution)/shard_map/all_to_all | solution.py:110
  177.9 2.9 %copy.27 = f32[384,2,1024]{2,0,1:T(8,128)S(1)} copy(f32[384,2,1024]{2,1,0:T(2,128)} %all-to-all-done.1) | data formatting | bytes 6291456 | tf_op jit(solution)/shard_map/all_to_all | solution.py:110
  180.8 0.4 copy.28
  181.2 3.5 %copy.29 = f32[24,32,1024]{2,1,0:T(8,128)} copy(f32[24,32,1024]{2,0,1:T(8,128)S(1)} %bitcast.59) | data formatting | bytes 6291456
  (6 shorter events, 0.1 us)
Async XLA Ops:
  0.6 111.6 %copy-start = (bf16[1536,384]{1,0:T(8,128)(2,1)S(1)}, bf16[1536,384]{1,0:T(8,128)(2,1)}, u32[]{:S(2)}) copy-start(bf16[1536,384]{1,0:T(8,128)(2,1)} %param.17) | copy-start | bytes 3538948
  7.0 15.0 %collective-permute-start = (f32[1,24,1,1024]{3,1,2,0:T(8,128)S(1)}, f32[1,24,1,1024]{3,1,2,0:T(8,128)S(1)}, u32[]{:S(2)}, u32[]{:S(2)}) collective-permute-start(f32[1,24,1,1024]{3,1,2,0:T(8,128)S(1)} %get-tuple-element.23), channel_id=1, source_target_pairs={{1,0},{2,1},{3,2},{4,3},{5,4},{6,5},{7,6},{8,7},{9,8},{10,9},{11,1... | collective-permute-start | bytes 294920 | tf_op jit(solution)/shard_map/ppermute | solution.py:19
  15.2 9.5 %collective-permute-start.1 = (f32[1,24,1,1024]{3,1,2,0:T(8,128)S(1)}, f32[1,24,1,1024]{3,1,2,0:T(8,128)S(1)}, u32[]{:S(2)}, u32[]{:S(2)}) collective-permute-start(f32[1,24,1,1024]{3,1,2,0:T(8,128)S(1)} %get-tuple-element.24), channel_id=1, source_target_pairs={{0,1},{1,2},{2,3},{3,4},{4,5},{5,6},{6,7},{7,8},{8,9},{9,10},{10,1... | collective-permute-start | bytes 294920 | tf_op jit(solution)/shard_map/ppermute | solution.py:16
  17.2 1.0 copy-start.5
  18.2 3.8 %copy-start.7 = (s32[2,24]{1,0:T(2,128)S(1)}, s32[2,24]{1,0:T(2,128)}, u32[]{:S(2)}) copy-start(s32[2,24]{1,0:T(2,128)} %param.16) | copy-start | bytes 580
  18.2 6.5 %copy-start.1 = (f32[24,32,1024]{2,1,0:T(8,128)S(1)}, f32[24,32,1024]{2,1,0:T(8,128)}, u32[]{:S(2)}) copy-start(f32[24,32,1024]{2,1,0:T(8,128)} %param.10) | copy-start | bytes 9437188
  35.4 7.9 %collective-permute-start.2 = (f32[1,24,1,1024]{3,1,2,0:T(8,128)S(1)}, f32[1,24,1,1024]{3,1,2,0:T(8,128)S(1)}, u32[]{:S(2)}, u32[]{:S(2)}) collective-permute-start(f32[1,24,1,1024]{3,1,2,0:T(8,128)S(1)} %get-tuple-element.19), channel_id=1, source_target_pairs={{1,0},{2,1},{3,2},{4,3},{5,4},{6,5},{7,6},{8,7},{9,8},{10,9},{11,1... | collective-permute-start | bytes 294920 | tf_op jit(solution)/shard_map/ppermute | solution.py:19
  39.1 10.1 %collective-permute-start.3 = (f32[1,24,1,1024]{3,1,2,0:T(8,128)S(1)}, f32[1,24,1,1024]{3,1,2,0:T(8,128)S(1)}, u32[]{:S(2)}, u32[]{:S(2)}) collective-permute-start(f32[1,24,1,1024]{3,1,2,0:T(8,128)S(1)} %get-tuple-element.20), channel_id=1, source_target_pairs={{0,1},{1,2},{2,3},{3,4},{4,5},{5,6},{6,7},{7,8},{8,9},{9,10},{10,1... | collective-permute-start | bytes 294920 | tf_op jit(solution)/shard_map/ppermute | solution.py:16
  54.4 7.7 %copy-start.2 = (bf16[384,2,1024]{2,1,0:T(2,128)(2,1)S(1)}, bf16[384,2,1024]{2,1,0:T(2,128)(2,1)}, u32[]{:S(2)}) copy-start(bf16[384,2,1024]{2,1,0:T(2,128)(2,1)} %param.11) | copy-start | bytes 4718596
  54.5 46.1 %all-to-all-start = ((f32[24,32,1024]{2,0,1:T(8,128)}), f32[24,32,1024]{2,0,1:T(8,128)}, u32[]{:S(2)}, u32[]{:S(2)}) async-start(f32[24,32,1024]{2,0,1:T(8,128)} %fusion.7), calls=%async_computation | async-start | bytes 6291456 | tf_op jit(solution)/shard_map/all_to_all | solution.py:100
  62.1 1.6 copy-start.6
  106.6 2.1 %copy-start.4 = (bf16[384,1536]{1,0:T(8,128)(2,1)S(1)}, bf16[384,1536]{1,0:T(8,128)(2,1)}, u32[]{:S(2)}) copy-start(bf16[384,1536]{1,0:T(8,128)(2,1)} %param.18) | copy-start | bytes 3538948
  108.7 3.5 %copy-start.3 = (bf16[48,8,2,1024]{3,1,2,0:T(8,128)(2,1)S(1)}, bf16[48,8,2,1024]{3,1,2,0:T(8,128)(2,1)}, u32[]{:S(2)}) copy-start(bf16[48,8,2,1024]{3,1,2,0:T(8,128)(2,1)} %copy.30) | copy-start | bytes 4718596
  108.7 3.5 %copy-start.8 = (f32[1536]{0:T(1024)S(1)}, f32[1536]{0:T(1024)}, u32[]{:S(2)}) copy-start(f32[1536]{0:T(1024)} %param.19) | copy-start | bytes 18436
  134.3 43.6 %all-to-all-start.1 = ((f32[384,2,1024]{2,1,0:T(2,128)}), f32[384,2,1024]{2,1,0:T(2,128)}, u32[]{:S(2)}, u32[]{:S(2)}) async-start(f32[384,2,1024]{2,1,0:T(2,128)} %copy.26), calls=%async_computation.1 | async-start | bytes 6291456 | tf_op jit(solution)/shard_map/all_to_all | solution.py:110
where the time goes:
time: 185 us
  waiting for transfers between devices  83.4 us (45%)
  local copies, waits for them, and re-layouts  29.6 us (16%)
  starting transfers between devices  29.2 us (16%)
  other arithmetic  27.2 us (15%)
  matrix products  14.3 us (8%)
    all_to_all x1, waiting for transfers between devices, shards(): lax.all_to_all(cell_start, 'comp', split_axis=0, concat_axis=1, tiled=True)  37.9 us
    all_to_all x1, waiting for transfers between devices, shards(): lax.all_to_all(costate, 'comp', split_axis=1, concat_axis=0, tiled=True)  36.8 us
    mul x2, other arithmetic, adjoint_step(): flux_x = cour_x * masked  13.6 us
    ppermute x2, starting transfers between devices, extended(): lax.ppermute(lax.slice_in_dim(block, 0, width, axis=dim), axis, backward)  11.9 us
    ppermute x2, waiting for transfers between devices, extended(): lax.ppermute(lax.slice_in_dim(block, block.shape[dim] - width, None, axis...  8.64 us
    all_to_all x1, starting transfers between devices, shards(): lax.all_to_all(costate, 'comp', split_axis=1, concat_axis=0, tiled=True)  7.64 us
    dot_general x1, matrix products, source_adjoint(): jnp.dot(w_in, cell_state, preferred_element_type=jnp.float32)  5.62 us
    unnamed x22, local copies, waits for them, and re-layouts  5.59 us
  transfers between devices with their start and end apart: 6, of which 4 were waited for; matrix products, arithmetic and copies ran while one was open for 5% of the time, Pallas kernels for 0%

commit v1 on v0

v1 whole, which is shorter than its diff:
```python
import functools
import math

import jax
import jax.numpy as jnp
import numpy as np
from jax import lax
from jax.experimental import pallas as pl
from jax.experimental.pallas import tpu as pltpu
from jax.sharding import PartitionSpec as P

MESH = pl.DeviceIdType.MESH
DIRS = 24
LANES = 128
ROWS = 32
RING = 40
TILES = 8
CHUNKS = 4
PER = TILES // CHUNKS
WIDE = PER * LANES
HID = 1536
BLOCK = 256
COMPS = 384
F32 = jnp.float32
BF16 = jnp.bfloat16


def iota(shape, dim):
    return lax.broadcasted_iota(jnp.int32, shape, dim)


def picks(mask):
    return jnp.where(mask, 1.0, 0.0).astype(BF16)


def decode(code):
    mask = jnp.where(code >= 64.0, 1.0, 0.0)
    rest = code - 64.0 * mask
    turn = jnp.floor(rest * 0.125)
    group = rest - 8.0 * turn
    celerity = 0.1 + 0.8 * group / 7.0
    turning = 0.3 * jnp.abs(turn - 3.5) / 3.5
    return mask, celerity * mask, turning * mask, turn


def kernel(
    n, slabs,
    forcing, fs, w_in_hbm, w_out_hbm, wind, cg, turn, sea, ww, sign, along,
    out, wgrad,
    C4, D4, Q0, Q1, CM, TM, MK, TN,
    HS, HR, MS, MR, S, R, IS, IR,
    FS, w_in, w_out, E, WT, A, G, WH, WW, WG,
    load_sem, w_sem, hs_sem, hr_sem, ms_sem, mr_sem, s1, r1, s2, r2, out_sem,
):
    me = lax.axis_index("comp")
    slab = lax.axis_index("space")
    C = C4.reshape(TILES, DIRS * RING, LANES)
    D = D4.reshape(TILES, DIRS * RING, LANES)
    FS2 = FS.reshape(2 * COMPS, TILES * LANES)

    def load(t):
        return pltpu.make_async_copy(
            forcing.at[:, :, pl.ds(t * LANES, LANES)], C4.at[t, :, pl.ds(0, ROWS), :], load_sem.at[t]
        )

    for t in range(TILES):
        load(t).start()
    weights = [
        pltpu.make_async_copy(fs, FS, w_sem.at[0]),
        pltpu.make_async_copy(w_in_hbm, w_in, w_sem.at[1]),
        pltpu.make_async_copy(w_out_hbm, w_out, w_sem.at[2]),
    ]
    for copy in weights:
        copy.start()

    barrier = pltpu.get_barrier_semaphore()

    def greet(step, carry):
        pl.semaphore_signal(
            barrier, inc=1, device_id={"comp": lax.rem(me + step, n)}, device_id_type=MESH
        )
        return carry

    lax.fori_loop(1, n, greet, 0)
    has_prev = slab > 0
    has_next = slab < slabs - 1

    @pl.when(has_prev)
    def _():
        pl.semaphore_signal(barrier, inc=1, device_id={"space": slab - 1}, device_id_type=MESH)

    @pl.when(has_next)
    def _():
        pl.semaphore_signal(barrier, inc=1, device_id={"space": slab + 1}, device_id_type=MESH)

    def code_of(rows):
        return (cg[0, rows, :] + 8 * turn[0, rows, :] + 64 * sea[rows, :]).astype(F32)

    MS[0] = code_of(slice(0, 2))
    MS[1] = code_of(slice(ROWS - 2, ROWS))

    def packed(t, row):
        first = C[t, pl.ds(row, DIRS, stride=RING), :]
        second = C[t, pl.ds(row + 1, DIRS, stride=RING), :]
        mixed = jnp.concatenate([first[16:], second[16:]], axis=0)
        return first[:16].astype(BF16), second[:16].astype(BF16), mixed.astype(BF16)

    def halo_copies(h, side):
        peer = slab - 1 if side == 0 else slab + 1
        return pltpu.make_async_remote_copy(
            src_ref=HS.at[h, side], dst_ref=HR.at[h, 1 - side],
            send_sem=hs_sem.at[h, side], recv_sem=hr_sem.at[h, 1 - side],
            device_id={"space": peer}, device_id_type=MESH,
        )

    def meta_copies(side):
        peer = slab - 1 if side == 0 else slab + 1
        return pltpu.make_async_remote_copy(
            src_ref=MS.at[side], dst_ref=MR.at[1 - side],
            send_sem=ms_sem.at[side], recv_sem=mr_sem.at[1 - side],
            device_id={"space": peer}, device_id_type=MESH,
        )

    def halo_arrived(h, side):
        peer = slab - 1 if side == 0 else slab + 1
        return pltpu.make_async_remote_copy(
            src_ref=HS.at[h, side], dst_ref=HR.at[h, side],
            send_sem=hs_sem.at[h, side], recv_sem=hr_sem.at[h, side],
            device_id={"space": peer}, device_id_type=MESH,
        )

    def meta_arrived(side):
        peer = slab - 1 if side == 0 else slab + 1
        return pltpu.make_async_remote_copy(
            src_ref=MS.at[side], dst_ref=MR.at[side],
            send_sem=ms_sem.at[side], recv_sem=mr_sem.at[side],
            device_id={"space": peer}, device_id_type=MESH,
        )

    for h in range(CHUNKS):
        for k in range(PER):
            t = h * PER + k
            load(t).wait()
            lanes = pl.ds(k * LANES, LANES)
            for side, row in ((0, 0), (1, ROWS - 2)):
                for part, value in enumerate(packed(t, row)):
                    HS[h, side, part, :, lanes] = value
        if h == 0:
            pl.semaphore_wait(barrier, n - 1 + has_prev.astype(jnp.int32) + has_next.astype(jnp.int32))
        for side, there in ((0, has_prev), (1, has_next)):

            @pl.when(there)
            def _(side=side, h=h):
                if h == 0:
                    meta_copies(side).start()
                halo_copies(h, side).start()

    for side, there in ((0, has_prev), (1, has_next)):

        @pl.when(jnp.logical_not(there))
        def _(side=side):
            MR[side] = jnp.zeros((2, TILES * LANES), F32)
            HR[:, side] = jnp.zeros((CHUNKS, 3, 16, WIDE), BF16)

    def levels(t, rows, code):
        mask, flow, turns, level = decode(code)
        MK[t, rows, :] = mask
        CM[t, rows, :] = flow
        TM[t, rows, :] = turns
        TN[t, rows, :] = level

    for t in range(TILES):
        lanes = slice(t * LANES, (t + 1) * LANES)
        code = (cg[0, :, lanes] + 8 * turn[0, :, lanes] + 64 * sea[:, lanes]).astype(F32)
        levels(t, slice(0, ROWS), code)

    def clear(d, carry):
        rows = pl.ds(pl.multiple_of(d * RING, 8), RING)
        zero = jnp.zeros((RING, LANES), F32)
        for q in (Q0, Q1):
            q[0, rows, :] = zero
            q[TILES + 1, rows, :] = zero
        return carry

    lax.fori_loop(0, DIRS, clear, 0)

    def weigh(t, carry):
        flow = CM[t, 0:ROWS, :]

        def one(d, carry):
            rows = pl.ds(pl.multiple_of(d * RING, 8), ROWS)
            Q0[t + 1, rows, :] = flow * C[t, rows, :]
            return carry

        return lax.fori_loop(0, DIRS, one, carry, unroll=4)

    lax.fori_loop(0, TILES, weigh, 0)

    for side, there in ((0, has_prev), (1, has_next)):

        @pl.when(there)
        def _(side=side):
            meta_arrived(side).wait_recv()

    for t in range(TILES):
        lanes = slice(t * LANES, (t + 1) * LANES)
        blank = jnp.zeros((4, LANES), F32)
        code = jnp.concatenate([MR[1, :, lanes], blank, MR[0, :, lanes]], axis=0)
        levels(t, slice(ROWS, RING), code)

    def take_halo(h):
        for side, there in ((0, has_prev), (1, has_next)):

            @pl.when(there)
            def _(side=side):
                halo_arrived(h, side).wait_recv()

        for k in range(PER):
            t = h * PER + k
            lanes = pl.ds(k * LANES, LANES)
            for side, row in ((0, RING - 2), (1, ROWS)):
                parts = [HR[h, side, part, :, lanes].astype(F32) for part in range(3)]
                for i in range(2):
                    value = jnp.concatenate([parts[i], parts[2][8 * i : 8 * i + 8]], axis=0)
                    C[t, pl.ds(row + i, DIRS, stride=RING), :] = value
            zero = jnp.zeros((DIRS, LANES), F32)
            for i in range(ROWS + 2, RING - 2):
                C[t, pl.ds(i, DIRS, stride=RING), :] = zero
            flow = CM[t, ROWS:RING, :]

            def one(d, carry):
                rows = pl.ds(pl.multiple_of(d * RING + ROWS, 8), RING - ROWS)
                Q0[t + 1, rows, :] = flow * C[t, rows, :]
                return carry

            lax.fori_loop(0, DIRS, one, 0, unroll=4)

    lane = iota((RING, LANES), 1)
    at_first = lane == 0
    at_last = lane == LANES - 1

    def step(t, state, q, result, next_q):
        flow = CM[t]
        turns = TM[t]
        mask = MK[t]
        up = TN[t] >= 4.0

        def one(d, carry):
            rows = pl.ds(pl.multiple_of(d * RING, 8), RING)
            above = pl.ds(pl.multiple_of(lax.rem(d + 1, DIRS) * RING, 8), RING)
            below = pl.ds(pl.multiple_of(lax.rem(d + DIRS - 1, DIRS) * RING, 8), RING)
            ax, ay = along[0, d], along[1, d]
            right = ax * (0.5 + 0.5 * sign[0, d].astype(F32))
            left = ax - right
            north = ay * (0.5 + 0.5 * sign[1, d].astype(F32))
            south = ay - north
            c = state[t, rows, :]
            here = q[t + 1, rows, :]
            from_right = pltpu.roll(jnp.where(at_first, q[t + 2, rows, :], here), LANES - 1, 1)
            from_left = pltpu.roll(jnp.where(at_last, q[t, rows, :], here), 1, 1)
            from_north = pltpu.roll(here, RING - 1, 0)
            from_south = pltpu.roll(here, 1, 0)
            turned = turns * (jnp.where(up, state[t, above, :], state[t, below, :]) - c)
            new = (
                mask * c
                + turned
                + (right * from_right + left * from_left)
                + (north * from_north + south * from_south)
                - (ax + ay) * here
            )
            if next_q is None:
                result[t, pl.ds(pl.multiple_of(d * RING, 8), ROWS), :] = new[:ROWS]
            else:
                result[t, rows, :] = new
                next_q[t + 1, rows, :] = flow * new
            return carry

        lax.fori_loop(0, DIRS, one, 0, unroll=4)

    def first_step(t, carry):
        step(t, C, Q0, D, Q1)
        return carry

    def second_step(t, carry):
        step(t, D, Q1, C, None)
        return carry

    def rows_of(p):
        return pl.ds(pl.multiple_of(p * 16, 16), 16)

    def exchange(h, p, source, target, send, recv):
        return pltpu.make_async_remote_copy(
            src_ref=source.at[h, :, rows_of(p), :], dst_ref=target.at[h, :, rows_of(me), :],
            send_sem=send.at[h, p], recv_sem=recv.at[h, me],
            device_id={"comp": p}, device_id_type=MESH,
        )

    def arrival(h, p, source, target, send, recv):
        return pltpu.make_async_remote_copy(
            src_ref=source.at[h, :, rows_of(me), :], dst_ref=target.at[h, :, rows_of(p), :],
            send_sem=send.at[h, p], recv_sem=recv.at[h, p],
            device_id={"comp": p}, device_id_type=MESH,
        )

    def own(h, source, target, recv):
        return pltpu.make_async_copy(
            source.at[h, :, rows_of(me), :], target.at[h, :, rows_of(me), :], recv.at[h, me]
        )

    def pack_for(h, p):
        for k in range(PER):
            lanes = pl.ds(k * LANES, LANES)
            for part, value in enumerate(packed(h * PER + k, 2 * p)):
                S[h, part, rows_of(p), lanes] = value

    take_halo(0)
    first_step(0, 0)

    def propagate(h, carry):
        @pl.when(h < CHUNKS - 1)
        def _():
            take_halo(h + 1)

        lax.fori_loop(h * PER + 1, jnp.minimum(h * PER + PER + 1, TILES), first_step, 0)
        lax.fori_loop(h * PER, h * PER + PER, second_step, 0)

        def send(i, carry):
            p = lax.rem(me + i, n)
            pack_for(h, p)
            exchange(h, p, S, R, s1, r1).start()
            return carry

        lax.fori_loop(1, n, send, 0)
        pack_for(h, me)
        own(h, S, R, r1).start()
        return carry

    lax.fori_loop(0, CHUNKS, propagate, 0)

    for copy in weights:
        copy.wait()
    wide = (COMPS, 2 * COMPS)
    for r in range(2):
        E[r] = picks(iota(wide, 1) == 2 * iota(wide, 0) + r)

    square = (COMPS, COMPS)
    place = iota(square, 0)
    rest = place - 256
    comp = jnp.where(
        place < 256,
        24 * lax.shift_right_logical(place, 4) + (place & 15),
        24 * lax.shift_right_arithmetic(rest, 3) + 16 + (rest & 7),
    )
    order = picks(iota(square, 1) == comp)
    nt = (((1,), (1,)), ((), ()))
    for m in range(HID // BLOCK):
        A[:, m * BLOCK : (m + 1) * BLOCK] = lax.dot_general(
            order, w_in[m * BLOCK : (m + 1) * BLOCK, :], nt, preferred_element_type=F32
        ).astype(BF16)

    tall = (COMPS, 512)
    place = iota(tall, 1)
    within = place & 15
    base = 24 * lax.shift_right_logical(place & 255, 4)
    eye = picks(iota((BLOCK, BLOCK), 0) == iota((BLOCK, BLOCK), 1))
    for r in range(2):
        mixed = jnp.where(
            lax.shift_right_logical(within, 3) == r, base + 16 + (within & 7), -1
        )
        chosen = picks(iota(tall, 0) == jnp.where(place < 256, base + within, mixed))
        for m in range(HID // BLOCK):
            turned = lax.dot_general(
                eye, w_out[:, m * BLOCK : (m + 1) * BLOCK], nt, preferred_element_type=F32
            ).astype(BF16)
            WT[r, m * BLOCK : (m + 1) * BLOCK, :] = jnp.dot(
                turned, chosen, preferred_element_type=F32
            ).astype(BF16)

    for b in range(HID // LANES):
        row = ww[0:1, b * LANES : (b + 1) * LANES]
        WW[b * LANES : (b + 1) * LANES, :] = jnp.broadcast_to(row, (LANES, LANES)).T

    def block_rows(m):
        return pl.ds(pl.multiple_of(m * BLOCK, BLOCK), BLOCK)

    def slopes(m, carry):
        rows = block_rows(m)
        winds = jnp.concatenate([WW[rows, :]] * PER, axis=1)
        for r in range(2):
            spread = jnp.dot(w_in[rows, :], E[r], preferred_element_type=F32).astype(BF16)
            for h in range(CHUNKS):
                lanes = slice(h * WIDE, (h + 1) * WIDE)
                squash = jnp.tanh(
                    jnp.dot(spread, FS2[:, lanes], preferred_element_type=F32)
                    + winds * wind[r : r + 1, lanes]
                )
                G[h, r, rows, :] = 1.0 - squash * squash
        return carry

    lax.fori_loop(0, HID // BLOCK, slopes, 0)

    def arrived(h, source, target, send, recv):
        def one(i, carry):
            arrival(h, lax.rem(me + n - i, n), source, target, send, recv).wait_recv()
            return carry

        lax.fori_loop(1, n, one, 0)
        own(h, source, target, recv).wait()

    def network(h, carry):
        arrived(h, S, R, s1, r1)
        tails = []
        for r in range(2):
            cells = jnp.concatenate([R[h, r], R[h, 2]], axis=0)

            def block(m, total):
                rows = block_rows(m)
                pulled = jnp.dot(WT[r, rows, :], cells, preferred_element_type=F32)
                weighted = G[h, r, rows, :] * pulled
                WH[rows, :] = weighted.astype(BF16)
                winds = jnp.concatenate([WW[rows, :]] * PER, axis=1)
                return total + jnp.sum((winds * weighted).reshape(BLOCK // 8, 8, WIDE), axis=0)

            total = lax.fori_loop(0, HID // BLOCK, block, jnp.zeros((8, WIDE), F32))
            WG[h, r : r + 1, :] = jnp.sum(total, axis=0, keepdims=True)
            increment = jnp.dot(A[...], WH[...], preferred_element_type=F32)
            IS[h, r] = increment[:256].astype(BF16)
            tails.append(increment[256:].reshape(16, 1, 8, WIDE))
        IS[h, 2] = jnp.concatenate(tails, axis=1).reshape(256, WIDE).astype(BF16)

        def send(i, carry):
            exchange(h, lax.rem(me + i, n), IS, IR, s2, r2).start()
            return carry

        lax.fori_loop(1, n, send, 0)
        own(h, IS, IR, r2).start()
        return carry

    lax.fori_loop(0, CHUNKS, network, 0)

    for h in range(CHUNKS):
        wgrad[:, h * WIDE : (h + 1) * WIDE] = WG[h]

    def store(t):
        return pltpu.make_async_copy(
            C4.at[t, :, pl.ds(0, ROWS), :], out.at[:, :, pl.ds(t * LANES, LANES)], out_sem.at[t]
        )

    for h in range(CHUNKS):
        arrived(h, IS, IR, s2, r2)

        def add(p, carry):
            for k in range(PER):
                lanes = pl.ds(k * LANES, LANES)
                parts = [IR[h, part, rows_of(p), lanes].astype(F32) for part in range(3)]
                for r in range(2):
                    value = jnp.concatenate([parts[r], parts[2][8 * r : 8 * r + 8]], axis=0)
                    rows = pl.ds(2 * p + r, DIRS, stride=RING)
                    C[h * PER + k, rows, :] = C[h * PER + k, rows, :] + value
            return carry

        lax.fori_loop(0, n, add, 0)
        for k in range(PER):
            store(h * PER + k).start()

    for t in range(TILES):
        store(t).wait()

    def sent(i, carry):
        p = lax.rem(me + i, n)
        for h in range(CHUNKS):
            exchange(h, p, S, R, s1, r1).wait_send()
            exchange(h, p, IS, IR, s2, r2).wait_send()
        return carry

    lax.fori_loop(1, n, sent, 0)
    for side, there in ((0, has_prev), (1, has_next)):

        @pl.when(there)
        def _(side=side):
            meta_copies(side).wait_send()
            for h in range(CHUNKS):
                halo_copies(h, side).wait_send()


def shards(n, slabs, forcing, state, wind, cg, turn, sea, sign, w_in, w_out, ww):
    angle = (np.arange(DIRS) + 0.5) * (2.0 * math.pi / DIRS)
    along = jnp.asarray(
        np.stack([0.5 * np.abs(np.cos(angle)), 0.5 * np.abs(np.sin(angle))]).astype(np.float32)
    )
    hbm = pl.BlockSpec(memory_space=pl.ANY)
    vmem = pl.BlockSpec(memory_space=pltpu.VMEM)
    smem = pl.BlockSpec(memory_space=pltpu.SMEM)
    sems = pltpu.SemaphoreType.DMA
    field = (TILES, DIRS, RING, LANES)
    fluxes = (TILES + 2, DIRS * RING, LANES)
    cells = (TILES, RING, LANES)
    message = (CHUNKS, 3, 16 * n, WIDE)
    return pl.pallas_call(
        functools.partial(kernel, n, slabs),
        out_shape=(
            jax.ShapeDtypeStruct(forcing.shape, F32),
            jax.ShapeDtypeStruct(wind.shape, F32),
        ),
        in_specs=[hbm] * 4 + [vmem] * 5 + [smem] * 2,
        out_specs=(hbm, vmem),
        scratch_shapes=[
            pltpu.VMEM(field, F32),
            pltpu.VMEM(field, F32),
            pltpu.VMEM(fluxes, F32),
            pltpu.VMEM(fluxes, F32),
            pltpu.VMEM(cells, F32),
            pltpu.VMEM(cells, F32),
            pltpu.VMEM(cells, F32),
            pltpu.VMEM(cells, F32),
            pltpu.VMEM((CHUNKS, 2, 3, 16, WIDE), BF16),
            pltpu.VMEM((CHUNKS, 2, 3, 16, WIDE), BF16),
            pltpu.VMEM((2, 2, TILES * LANES), F32),
            pltpu.VMEM((2, 2, TILES * LANES), F32),
            pltpu.VMEM(message, BF16),
            pltpu.VMEM(message, BF16),
            pltpu.VMEM(message, BF16),
            pltpu.VMEM(message, BF16),
            pltpu.VMEM(state.shape, BF16),
            pltpu.VMEM(w_in.shape, BF16),
            pltpu.VMEM(w_out.shape, BF16),
            pltpu.VMEM((2, COMPS, 2 * COMPS), BF16),
            pltpu.VMEM((2, HID, 512), BF16),
            pltpu.VMEM((COMPS, HID), BF16),
            pltpu.VMEM((CHUNKS, 2, HID, WIDE), F32),
            pltpu.VMEM((HID, WIDE), BF16),
            pltpu.VMEM((HID, LANES), F32),
            pltpu.VMEM((CHUNKS, 2, WIDE), F32),
            sems((TILES,)),
            sems((3,)),
            sems((CHUNKS, 2)),
            sems((CHUNKS, 2)),
            sems((2,)),
            sems((2,)),
            sems((CHUNKS, n)),
            sems((CHUNKS, n)),
            sems((CHUNKS, n)),
            sems((CHUNKS, n)),
            sems((TILES,)),
        ],
        compiler_params=pltpu.CompilerParams(
            collective_id=0, has_side_effects=True, vmem_limit_bytes=58 << 20
        ),
        name="adjoint_window",
    )(forcing, state, w_in, w_out, wind, cg, turn, sea, ww.reshape(1, -1), sign, along)


def solution(mesh):
    placed = (
        P("comp", "space", None),
        P(None, ("space", "comp"), None),
        P(("space", "comp"), None),
        P("comp", "space", None),
        P("comp", "space", None),
        P("space", None),
        P(),
        P(),
        P(),
        P(),
    )
    return jax.shard_map(
        functools.partial(shards, mesh.shape["comp"], mesh.shape["space"]),
        mesh=mesh,
        in_specs=placed,
        out_specs=(P("comp", "space", None), P(("space", "comp"), None)),
        check_vma=False,
    )
```

time: 185 us -> 74.6 us (0.40)
  waiting for transfers between devices: 83.4 us -> 0 us
  Pallas kernels: 0 us -> 68 us
  starting transfers between devices: 29.2 us -> 0 us
  other arithmetic: 27.2 us -> 0 us
  local copies, waits for them, and re-layouts: 29.6 us -> 5.87 us
  matrix products: 14.3 us -> 0 us
    all_to_all x2 -> x0, waiting for transfers between devices: 74.7 us -> none  [the longest x1 37.9 us: shards(): lax.all_to_all(cell_start, 'comp', split_axis=0, concat_axis=1, tiled=True)]
    pallas_call x0 -> x1, Pallas kernels: none -> 68 us  [shards(): pl.pallas_call(functools.partial(kernel, n, slabs), out_shape=(jax.ShapeD...]
    ppermute x4 -> x0, starting transfers between devices: 16.5 us -> none  [the longest x2 11.9 us: extended(): lax.ppermute(lax.slice_in_dim(block, 0, width, axis=dim), axis, backward)]
    dot_general x3 -> x0, matrix products: 14.3 us -> none  [the longest x1 5.62 us: source_adjoint(): jnp.dot(w_in, cell_state, preferred_element_type=jnp.float32)]
    mul x4 -> x0, other arithmetic: 14.3 us -> none  [the longest x2 13.6 us: adjoint_step(): flux_x = cour_x * masked]
    all_to_all x2 -> x0, starting transfers between devices: 12.7 us -> none  [the longest x1 7.64 us: shards(): lax.all_to_all(costate, 'comp', split_axis=1, concat_axis=0, tiled=True)]
    ppermute x4 -> x0, waiting for transfers between devices: 8.64 us -> none  [the longest x2 8.64 us: extended(): lax.ppermute(lax.slice_in_dim(block, block.shape[dim] - width, None, axis...]
    all_to_all x3 -> x0, local copies, waits for them, and re-layouts: 7.24 us -> none  [the longest x1 3.94 us: shards(): lax.all_to_all(costate, 'comp', split_axis=1, concat_axis=0, tiled=True)]
  transfers between devices with their start and end apart: 6 -> 0, of which waited for: 4 -> 0; matrix products, arithmetic and copies ran while one was open for 5% -> 0% of each run, Pallas kernels for 0% -> 0%
where the time goes in v1:
time: 74.6 us; the launch traced here: 74.5 us
  Pallas kernels  68 us (91%)
  local copies, waits for them, and re-layouts  5.87 us (8%)
    pallas_call x1, Pallas kernels, shards(): pl.pallas_call(functools.partial(kernel, n, slabs), out_shape=(jax.ShapeD...  68 us
    unnamed x4, local copies, waits for them, and re-layouts  4.58 us

profile of v1, /device:TPU:7, one launch (start us, length us, event | category | flops | bytes accessed | tf_op | source)
XLA Modules:
  0.0 74.5 jit_solution(17446993814668447588)
XLA Ops:
  0.6 1.3 %reshape.7.ww = f32[1,1536]{1,0:T(1,128)} reshape(f32[1536]{0:T(1024)} %param.20) | data formatting | bytes 12288 | tf_op jit(solution)/shard_map/reshape | solution.py:550
  1.9 68.0 %adjoint_window.1 = (f32[24,32,1024]{2,1,0:T(8,128)}, f32[2,1024]{1,0:T(2,128)}) custom-call(f32[24,32,1024]{2,1,0:T(8,128)} %forcing.1, bf16[384,2,1024]{2,1,0:T(2,128)(2,1)} %fs.1, bf16[1536,384]{1,0:T(8,128)(2,1)} %w_in_hbm.1, bf16[384,1536]{1,0:T(8,128)(2,1)} %w_out_hbm.1, f32[2,1024]{1,0:T(2,128)} %wind.1, s32[1,32,1024]{2,1,0:T(8,128)} %cg.1, ...), custom_call_target="tpu_custom_call" | custom-call | tf_op jit(solution)/shard_map/adjoint_window/pallas_call | solution.py:499
  69.9 0.0 copy-start
  69.9 4.0 %copy.15 = f32[24,32,1024]{2,1,0:T(8,128)} copy(f32[24,32,1024]{2,1,0:T(8,128)} %get-tuple-element.4) | data formatting | bytes 6291456
  73.9 0.0 copy-done
  73.9 0.6 copy.16
Async XLA Ops:
  69.9 4.0 %copy-start = (f32[2,1024]{1,0:T(2,128)S(1)}, f32[2,1024]{1,0:T(2,128)}, u32[]{:S(2)}) copy-start(f32[2,1024]{1,0:T(2,128)} %get-tuple-element.5) | copy-start | bytes 24580

commit v2 on v1

--- a/solution.py
+++ b/solution.py
@@ -45,18 +45,17 @@
 
 def kernel(
     n, slabs,
-    forcing, fs, w_in_hbm, w_out_hbm, wind, cg, turn, sea, ww, sign, along,
+    forcing, fs, w_in_hbm, w_out_hbm, cg_hbm, turn_hbm, sea_hbm, wind_hbm, ww_hbm, sign, along,
     out, wgrad,
     C4, D4, Q0, Q1, CM, TM, MK, TN,
     HS, HR, MS, MR, S, R, IS, IR,
-    FS, w_in, w_out, E, WT, A, G, WH, WW, WG,
+    cg, turn, sea, wind, ww, FS4, w_in, w_out, E, WT, A, G, WH, WW, WG,
     load_sem, w_sem, hs_sem, hr_sem, ms_sem, mr_sem, s1, r1, s2, r2, out_sem,
 ):
     me = lax.axis_index("comp")
     slab = lax.axis_index("space")
     C = C4.reshape(TILES, DIRS * RING, LANES)
     D = D4.reshape(TILES, DIRS * RING, LANES)
-    FS2 = FS.reshape(2 * COMPS, TILES * LANES)
 
     def load(t):
         return pltpu.make_async_copy(
@@ -65,10 +64,24 @@
 
     for t in range(TILES):
         load(t).start()
+    FS = FS4.reshape(CHUNKS, 2 * COMPS, WIDE)
+    maps = [
+        pltpu.make_async_copy(cg_hbm.at[0], cg, w_sem.at[2]),
+        pltpu.make_async_copy(turn_hbm.at[0], turn, w_sem.at[3]),
+        pltpu.make_async_copy(sea_hbm, sea, w_sem.at[4]),
+    ]
+    for copy in maps:
+        copy.start()
     weights = [
-        pltpu.make_async_copy(fs, FS, w_sem.at[0]),
-        pltpu.make_async_copy(w_in_hbm, w_in, w_sem.at[1]),
-        pltpu.make_async_copy(w_out_hbm, w_out, w_sem.at[2]),
+        pltpu.make_async_copy(wind_hbm, wind, w_sem.at[5 + CHUNKS]),
+        pltpu.make_async_copy(ww_hbm, ww, w_sem.at[6 + CHUNKS]),
+        pltpu.make_async_copy(w_in_hbm, w_in, w_sem.at[0]),
+        pltpu.make_async_copy(w_out_hbm, w_out, w_sem.at[1]),
+    ] + [
+        pltpu.make_async_copy(
+            fs.at[:, :, pl.ds(h * WIDE, WIDE)], FS4.at[h], w_sem.at[5 + h]
+        )
+        for h in range(CHUNKS)
     ]
     for copy in weights:
         copy.start()
@@ -93,8 +106,11 @@
     def _():
         pl.semaphore_signal(barrier, inc=1, device_id={"space": slab + 1}, device_id_type=MESH)
 
+    for copy in maps:
+        copy.wait()
+
     def code_of(rows):
-        return (cg[0, rows, :] + 8 * turn[0, rows, :] + 64 * sea[rows, :]).astype(F32)
+        return (cg[rows, :] + 8 * turn[rows, :] + 64 * sea[rows, :]).astype(F32)
 
     MS[0] = code_of(slice(0, 2))
     MS[1] = code_of(slice(ROWS - 2, ROWS))
@@ -171,7 +187,7 @@
 
     for t in range(TILES):
         lanes = slice(t * LANES, (t + 1) * LANES)
-        code = (cg[0, :, lanes] + 8 * turn[0, :, lanes] + 64 * sea[:, lanes]).astype(F32)
+        code = (cg[:, lanes] + 8 * turn[:, lanes] + 64 * sea[:, lanes]).astype(F32)
         levels(t, slice(0, ROWS), code)
 
     def clear(d, carry):
@@ -236,8 +252,6 @@
             lax.fori_loop(0, DIRS, one, 0, unroll=4)
 
     lane = iota((RING, LANES), 1)
-    at_first = lane == 0
-    at_last = lane == LANES - 1
 
     def step(t, state, q, result, next_q):
         flow = CM[t]
@@ -250,21 +264,22 @@
             above = pl.ds(pl.multiple_of(lax.rem(d + 1, DIRS) * RING, 8), RING)
             below = pl.ds(pl.multiple_of(lax.rem(d + DIRS - 1, DIRS) * RING, 8), RING)
             ax, ay = along[0, d], along[1, d]
-            right = ax * (0.5 + 0.5 * sign[0, d].astype(F32))
-            left = ax - right
+            toward = sign[0, d]
             north = ay * (0.5 + 0.5 * sign[1, d].astype(F32))
             south = ay - north
             c = state[t, rows, :]
             here = q[t + 1, rows, :]
-            from_right = pltpu.roll(jnp.where(at_first, q[t + 2, rows, :], here), LANES - 1, 1)
-            from_left = pltpu.roll(jnp.where(at_last, q[t, rows, :], here), 1, 1)
+            edge = jnp.where(toward > 0, 0, LANES - 1)
+            shift = jnp.where(toward > 0, LANES - 1, 1)
+            beside = q[t + 1 + toward, rows, :]
+            from_side = pltpu.roll(jnp.where(lane == edge, beside, here), shift, 1)
             from_north = pltpu.roll(here, RING - 1, 0)
             from_south = pltpu.roll(here, 1, 0)
             turned = turns * (jnp.where(up, state[t, above, :], state[t, below, :]) - c)
             new = (
                 mask * c
                 + turned
-                + (right * from_right + left * from_left)
+                + ax * from_side
                 + (north * from_north + south * from_south)
                 - (ax + ay) * here
             )
@@ -275,7 +290,7 @@
                 next_q[t + 1, rows, :] = flow * new
             return carry
 
-        lax.fori_loop(0, DIRS, one, 0, unroll=4)
+        lax.fori_loop(0, DIRS, one, 0, unroll=True)
 
     def first_step(t, carry):
         step(t, C, Q0, D, Q1)
@@ -291,48 +306,39 @@
     def exchange(h, p, source, target, send, recv):
         return pltpu.make_async_remote_copy(
             src_ref=source.at[h, :, rows_of(p), :], dst_ref=target.at[h, :, rows_of(me), :],
-            send_sem=send.at[h, p], recv_sem=recv.at[h, me],
+            send_sem=send.at[h], recv_sem=recv.at[h],
             device_id={"comp": p}, device_id_type=MESH,
         )
 
-    def arrival(h, p, source, target, send, recv):
-        return pltpu.make_async_remote_copy(
-            src_ref=source.at[h, :, rows_of(me), :], dst_ref=target.at[h, :, rows_of(p), :],
-            send_sem=send.at[h, p], recv_sem=recv.at[h, p],
-            device_id={"comp": p}, device_id_type=MESH,
-        )
-
-    def own(h, source, target, recv):
-        return pltpu.make_async_copy(
-            source.at[h, :, rows_of(me), :], target.at[h, :, rows_of(me), :], recv.at[h, me]
-        )
-
-    def pack_for(h, p):
+    def all_of(h, buffer, sem):
+        others = buffer.at[h, :, pl.ds(0, 16 * (n - 1)), :]
+        return pltpu.make_async_copy(others, others, sem.at[h])
+
+    def pack_for(h, p, buffer):
         for k in range(PER):
             lanes = pl.ds(k * LANES, LANES)
             for part, value in enumerate(packed(h * PER + k, 2 * p)):
-                S[h, part, rows_of(p), lanes] = value
+                buffer[h, part, rows_of(p), lanes] = value
 
     take_halo(0)
-    first_step(0, 0)
 
     def propagate(h, carry):
         @pl.when(h < CHUNKS - 1)
         def _():
             take_halo(h + 1)
 
-        lax.fori_loop(h * PER + 1, jnp.minimum(h * PER + PER + 1, TILES), first_step, 0)
+        first = jnp.where(h == 0, 0, h * PER + 1)
+        lax.fori_loop(first, jnp.minimum(h * PER + PER + 1, TILES), first_step, 0)
         lax.fori_loop(h * PER, h * PER + PER, second_step, 0)
 
         def send(i, carry):
             p = lax.rem(me + i, n)
-            pack_for(h, p)
+            pack_for(h, p, S)
             exchange(h, p, S, R, s1, r1).start()
             return carry
 
         lax.fori_loop(1, n, send, 0)
-        pack_for(h, me)
-        own(h, S, R, r1).start()
+        pack_for(h, me, R)
         return carry
 
     lax.fori_loop(0, CHUNKS, propagate, 0)
@@ -363,52 +369,44 @@
     within = place & 15
     base = 24 * lax.shift_right_logical(place & 255, 4)
     eye = picks(iota((BLOCK, BLOCK), 0) == iota((BLOCK, BLOCK), 1))
+    chosen = []
     for r in range(2):
         mixed = jnp.where(
             lax.shift_right_logical(within, 3) == r, base + 16 + (within & 7), -1
         )
-        chosen = picks(iota(tall, 0) == jnp.where(place < 256, base + within, mixed))
-        for m in range(HID // BLOCK):
-            turned = lax.dot_general(
-                eye, w_out[:, m * BLOCK : (m + 1) * BLOCK], nt, preferred_element_type=F32
-            ).astype(BF16)
-            WT[r, m * BLOCK : (m + 1) * BLOCK, :] = jnp.dot(
-                turned, chosen, preferred_element_type=F32
-            ).astype(BF16)
+        chosen.append(picks(iota(tall, 0) == jnp.where(place < 256, base + within, mixed)))
+    for m in range(HID // BLOCK):
+        rows = slice(m * BLOCK, (m + 1) * BLOCK)
+        turned = lax.dot_general(eye, w_out[:, rows], nt, preferred_element_type=F32).astype(BF16)
+        for r in range(2):
+            WT[r, rows, :] = jnp.dot(turned, chosen[r], preferred_element_type=F32).astype(BF16)
 
     for b in range(HID // LANES):
-        row = ww[0:1, b * LANES : (b + 1) * LANES]
+        row = ww[b * LANES : (b + 1) * LANES].reshape(1, LANES)
         WW[b * LANES : (b + 1) * LANES, :] = jnp.broadcast_to(row, (LANES, LANES)).T
 
     def block_rows(m):
         return pl.ds(pl.multiple_of(m * BLOCK, BLOCK), BLOCK)
 
-    def slopes(m, carry):
-        rows = block_rows(m)
-        winds = jnp.concatenate([WW[rows, :]] * PER, axis=1)
+    def slopes(h):
         for r in range(2):
-            spread = jnp.dot(w_in[rows, :], E[r], preferred_element_type=F32).astype(BF16)
-            for h in range(CHUNKS):
-                lanes = slice(h * WIDE, (h + 1) * WIDE)
+            cells = jnp.dot(E[r], FS[h], preferred_element_type=F32).astype(BF16)
+            gusts = wind[r : r + 1, pl.ds(pl.multiple_of(h * WIDE, WIDE), WIDE)]
+
+            def block(m, carry):
+                rows = block_rows(m)
+                winds = jnp.concatenate([WW[rows, :]] * PER, axis=1)
                 squash = jnp.tanh(
-                    jnp.dot(spread, FS2[:, lanes], preferred_element_type=F32)
-                    + winds * wind[r : r + 1, lanes]
+                    jnp.dot(w_in[rows, :], cells, preferred_element_type=F32) + winds * gusts
                 )
-                G[h, r, rows, :] = 1.0 - squash * squash
-        return carry
-
-    lax.fori_loop(0, HID // BLOCK, slopes, 0)
-
-    def arrived(h, source, target, send, recv):
-        def one(i, carry):
-            arrival(h, lax.rem(me + n - i, n), source, target, send, recv).wait_recv()
-            return carry
-
-        lax.fori_loop(1, n, one, 0)
-        own(h, source, target, recv).wait()
+                G[r, rows, :] = 1.0 - squash * squash
+                return carry
+
+            lax.fori_loop(0, HID // BLOCK, block, 0, unroll=True)
 
     def network(h, carry):
-        arrived(h, S, R, s1, r1)
+        slopes(h)
+        all_of(h, R, r1).wait()
         tails = []
         for r in range(2):
             cells = jnp.concatenate([R[h, r], R[h, 2]], axis=0)
@@ -416,12 +414,14 @@
             def block(m, total):
                 rows = block_rows(m)
                 pulled = jnp.dot(WT[r, rows, :], cells, preferred_element_type=F32)
-                weighted = G[h, r, rows, :] * pulled
+                weighted = G[r, rows, :] * pulled
                 WH[rows, :] = weighted.astype(BF16)
                 winds = jnp.concatenate([WW[rows, :]] * PER, axis=1)
                 return total + jnp.sum((winds * weighted).reshape(BLOCK // 8, 8, WIDE), axis=0)
 
-            total = lax.fori_loop(0, HID // BLOCK, block, jnp.zeros((8, WIDE), F32))
+            total = lax.fori_loop(
+                0, HID // BLOCK, block, jnp.zeros((8, WIDE), F32), unroll=True
+            )
             WG[h, r : r + 1, :] = jnp.sum(total, axis=0, keepdims=True)
             increment = jnp.dot(A[...], WH[...], preferred_element_type=F32)
             IS[h, r] = increment[:256].astype(BF16)
@@ -433,7 +433,7 @@
             return carry
 
         lax.fori_loop(1, n, send, 0)
-        own(h, IS, IR, r2).start()
+        IR[h, :, rows_of(me), :] = IS[h, :, rows_of(me), :]
         return carry
 
     lax.fori_loop(0, CHUNKS, network, 0)
@@ -447,7 +447,7 @@
         )
 
     for h in range(CHUNKS):
-        arrived(h, IS, IR, s2, r2)
+        all_of(h, IR, r2).wait()
 
         def add(p, carry):
             for k in range(PER):
@@ -466,14 +466,9 @@
     for t in range(TILES):
         store(t).wait()
 
-    def sent(i, carry):
-        p = lax.rem(me + i, n)
-        for h in range(CHUNKS):
-            exchange(h, p, S, R, s1, r1).wait_send()
-            exchange(h, p, IS, IR, s2, r2).wait_send()
-        return carry
-
-    lax.fori_loop(1, n, sent, 0)
+    for h in range(CHUNKS):
+        all_of(h, S, s1).wait()
+        all_of(h, IS, s2).wait()
     for side, there in ((0, has_prev), (1, has_next)):
 
         @pl.when(there)
@@ -502,7 +497,7 @@
             jax.ShapeDtypeStruct(forcing.shape, F32),
             jax.ShapeDtypeStruct(wind.shape, F32),
         ),
-        in_specs=[hbm] * 4 + [vmem] * 5 + [smem] * 2,
+        in_specs=[hbm] * 9 + [smem] * 2,
         out_specs=(hbm, vmem),
         scratch_shapes=[
             pltpu.VMEM(field, F32),
@@ -521,33 +516,38 @@
             pltpu.VMEM(message, BF16),
             pltpu.VMEM(message, BF16),
             pltpu.VMEM(message, BF16),
-            pltpu.VMEM(state.shape, BF16),
+            pltpu.VMEM((ROWS, TILES * LANES), jnp.int32),
+            pltpu.VMEM((ROWS, TILES * LANES), jnp.int32),
+            pltpu.VMEM((ROWS, TILES * LANES), jnp.int32),
+            pltpu.VMEM(wind.shape, F32),
+            pltpu.VMEM(ww.shape, F32),
+            pltpu.VMEM((CHUNKS, COMPS, 2, WIDE), BF16),
             pltpu.VMEM(w_in.shape, BF16),
             pltpu.VMEM(w_out.shape, BF16),
             pltpu.VMEM((2, COMPS, 2 * COMPS), BF16),
             pltpu.VMEM((2, HID, 512), BF16),
             pltpu.VMEM((COMPS, HID), BF16),
-            pltpu.VMEM((CHUNKS, 2, HID, WIDE), F32),
+            pltpu.VMEM((2, HID, WIDE), F32),
             pltpu.VMEM((HID, WIDE), BF16),
             pltpu.VMEM((HID, LANES), F32),
             pltpu.VMEM((CHUNKS, 2, WIDE), F32),
             sems((TILES,)),
-            sems((3,)),
+            sems((7 + CHUNKS,)),
             sems((CHUNKS, 2)),
             sems((CHUNKS, 2)),
             sems((2,)),
             sems((2,)),
-            sems((CHUNKS, n)),
-            sems((CHUNKS, n)),
-            sems((CHUNKS, n)),
-            sems((CHUNKS, n)),
+            sems((CHUNKS,)),
+            sems((CHUNKS,)),
+            sems((CHUNKS,)),
+            sems((CHUNKS,)),
             sems((TILES,)),
         ],
         compiler_params=pltpu.CompilerParams(
             collective_id=0, has_side_effects=True, vmem_limit_bytes=58 << 20
         ),
         name="adjoint_window",
-    )(forcing, state, w_in, w_out, wind, cg, turn, sea, ww.reshape(1, -1), sign, along)
+    )(forcing, state, w_in, w_out, cg, turn, sea, wind, ww, sign, along)
 
 
 def solution(mesh):

time: 74.6 us -> 59.2 us (0.79)
  Pallas kernels: 68 us -> 53.8 us
  local copies, waits for them, and re-layouts: 5.87 us -> 4.58 us
    pallas_call x1, Pallas kernels: 68 us -> 53.8 us  [shards(): pl.pallas_call(functools.partial(kernel, n, slabs), out_shape=(jax.ShapeD...]
    reshape x1 -> x0, local copies, waits for them, and re-layouts: 1.3 us -> none  [shards(): ww.reshape(1, -1)]
where the time goes in v2:
time: 59.2 us; the launch traced here: 59 us
  Pallas kernels  53.8 us (91%)
  local copies, waits for them, and re-layouts  4.58 us (8%)
  between operations  0.65 us (1%)
    pallas_call x1, Pallas kernels, shards(): pl.pallas_call(functools.partial(kernel, n, slabs), out_shape=(jax.ShapeD...  53.8 us
    unnamed x4, local copies, waits for them, and re-layouts  4.58 us

profile of v2, /device:TPU:7, one launch (start us, length us, event | category | flops | bytes accessed | tf_op | source)
XLA Modules:
  0.0 59.0 jit_solution(9145528711636451767)
XLA Ops:
  0.6 53.8 %adjoint_window.1 = (f32[24,32,1024]{2,1,0:T(8,128)}, f32[2,1024]{1,0:T(2,128)}) custom-call(f32[24,32,1024]{2,1,0:T(8,128)} %forcing.1, bf16[384,2,1024]{2,1,0:T(2,128)(2,1)} %fs.1, bf16[1536,384]{1,0:T(8,128)(2,1)} %w_in_hbm.1, bf16[384,1536]{1,0:T(8,128)(2,1)} %w_out_hbm.1, s32[1,32,1024]{2,1,0:T(8,128)} %cg_hbm.1, s32[1,32,1024]{2,1,0:T(8,128)} %turn_hbm.1, ...), custom_call_target="tpu_custom_call" | custom-call | tf_op jit(solution)/shard_map/adjoint_window/pallas_call | solution.py:494
  54.4 0.0 copy-start
  54.5 4.0 %copy.15 = f32[24,32,1024]{2,1,0:T(8,128)} copy(f32[24,32,1024]{2,1,0:T(8,128)} %get-tuple-element.4) | data formatting | bytes 6291456
  58.4 0.0 copy-done
  58.4 0.6 %copy.16 = f32[2,1024]{1,0:T(2,128)} copy(f32[2,1024]{1,0:T(2,128)S(1)} %copy-done) | data formatting | bytes 16384
Async XLA Ops:
  54.4 4.0 %copy-start = (f32[2,1024]{1,0:T(2,128)S(1)}, f32[2,1024]{1,0:T(2,128)}, u32[]{:S(2)}) copy-start(f32[2,1024]{1,0:T(2,128)} %get-tuple-element.5) | copy-start | bytes 24580

commit v3 on v2

--- a/solution.py
+++ b/solution.py
@@ -33,24 +33,14 @@
     return jnp.where(mask, 1.0, 0.0).astype(BF16)
 
 
-def decode(code):
-    mask = jnp.where(code >= 64.0, 1.0, 0.0)
-    rest = code - 64.0 * mask
-    turn = jnp.floor(rest * 0.125)
-    group = rest - 8.0 * turn
-    celerity = 0.1 + 0.8 * group / 7.0
-    turning = 0.3 * jnp.abs(turn - 3.5) / 3.5
-    return mask, celerity * mask, turning * mask, turn
-
-
 def kernel(
     n, slabs,
     forcing, fs, w_in_hbm, w_out_hbm, cg_hbm, turn_hbm, sea_hbm, wind_hbm, ww_hbm, sign, along,
-    out, wgrad,
-    C4, D4, Q0, Q1, CM, TM, MK, TN,
-    HS, HR, MS, MR, S, R, IS, IR,
+    D4, wgrad,
+    C4, Q0, Q1, CM, TM, MK, TN, NO, SO,
+    HS, HR, S, R, IS, IR,
     cg, turn, sea, wind, ww, FS4, w_in, w_out, E, WT, A, G, WH, WW, WG,
-    load_sem, w_sem, hs_sem, hr_sem, ms_sem, mr_sem, s1, r1, s2, r2, out_sem,
+    load_sem, w_sem, hs_sem, hr_sem, s1, r1, s2, r2,
 ):
     me = lax.axis_index("comp")
     slab = lax.axis_index("space")
@@ -62,8 +52,6 @@
             forcing.at[:, :, pl.ds(t * LANES, LANES)], C4.at[t, :, pl.ds(0, ROWS), :], load_sem.at[t]
         )
 
-    for t in range(TILES):
-        load(t).start()
     FS = FS4.reshape(CHUNKS, 2 * COMPS, WIDE)
     maps = [
         pltpu.make_async_copy(cg_hbm.at[0], cg, w_sem.at[2]),
@@ -72,6 +60,8 @@
     ]
     for copy in maps:
         copy.start()
+    for t in range(TILES):
+        load(t).start()
     weights = [
         pltpu.make_async_copy(wind_hbm, wind, w_sem.at[5 + CHUNKS]),
         pltpu.make_async_copy(ww_hbm, ww, w_sem.at[6 + CHUNKS]),
@@ -83,8 +73,6 @@
         )
         for h in range(CHUNKS)
     ]
-    for copy in weights:
-        copy.start()
 
     barrier = pltpu.get_barrier_semaphore()
 
@@ -97,6 +85,7 @@
     lax.fori_loop(1, n, greet, 0)
     has_prev = slab > 0
     has_next = slab < slabs - 1
+    sides = ((0, has_prev), (1, has_next))
 
     @pl.when(has_prev)
     def _():
@@ -106,34 +95,14 @@
     def _():
         pl.semaphore_signal(barrier, inc=1, device_id={"space": slab + 1}, device_id_type=MESH)
 
-    for copy in maps:
-        copy.wait()
-
-    def code_of(rows):
-        return (cg[rows, :] + 8 * turn[rows, :] + 64 * sea[rows, :]).astype(F32)
-
-    MS[0] = code_of(slice(0, 2))
-    MS[1] = code_of(slice(ROWS - 2, ROWS))
-
-    def packed(t, row):
-        first = C[t, pl.ds(row, DIRS, stride=RING), :]
-        second = C[t, pl.ds(row + 1, DIRS, stride=RING), :]
-        mixed = jnp.concatenate([first[16:], second[16:]], axis=0)
-        return first[:16].astype(BF16), second[:16].astype(BF16), mixed.astype(BF16)
-
-    def halo_copies(h, side):
+    for copy in weights:
+        copy.start()
+
+    def halo_copy(h, side):
         peer = slab - 1 if side == 0 else slab + 1
         return pltpu.make_async_remote_copy(
             src_ref=HS.at[h, side], dst_ref=HR.at[h, 1 - side],
             send_sem=hs_sem.at[h, side], recv_sem=hr_sem.at[h, 1 - side],
-            device_id={"space": peer}, device_id_type=MESH,
-        )
-
-    def meta_copies(side):
-        peer = slab - 1 if side == 0 else slab + 1
-        return pltpu.make_async_remote_copy(
-            src_ref=MS.at[side], dst_ref=MR.at[1 - side],
-            send_sem=ms_sem.at[side], recv_sem=mr_sem.at[1 - side],
             device_id={"space": peer}, device_id_type=MESH,
         )
 
@@ -145,50 +114,17 @@
             device_id={"space": peer}, device_id_type=MESH,
         )
 
-    def meta_arrived(side):
-        peer = slab - 1 if side == 0 else slab + 1
-        return pltpu.make_async_remote_copy(
-            src_ref=MS.at[side], dst_ref=MR.at[side],
-            send_sem=ms_sem.at[side], recv_sem=mr_sem.at[side],
-            device_id={"space": peer}, device_id_type=MESH,
-        )
-
-    for h in range(CHUNKS):
-        for k in range(PER):
-            t = h * PER + k
-            load(t).wait()
-            lanes = pl.ds(k * LANES, LANES)
-            for side, row in ((0, 0), (1, ROWS - 2)):
-                for part, value in enumerate(packed(t, row)):
-                    HS[h, side, part, :, lanes] = value
-        if h == 0:
-            pl.semaphore_wait(barrier, n - 1 + has_prev.astype(jnp.int32) + has_next.astype(jnp.int32))
-        for side, there in ((0, has_prev), (1, has_next)):
-
-            @pl.when(there)
-            def _(side=side, h=h):
-                if h == 0:
-                    meta_copies(side).start()
-                halo_copies(h, side).start()
-
-    for side, there in ((0, has_prev), (1, has_next)):
+    for side, there in sides:
 
         @pl.when(jnp.logical_not(there))
         def _(side=side):
-            MR[side] = jnp.zeros((2, TILES * LANES), F32)
             HR[:, side] = jnp.zeros((CHUNKS, 3, 16, WIDE), BF16)
 
-    def levels(t, rows, code):
-        mask, flow, turns, level = decode(code)
-        MK[t, rows, :] = mask
-        CM[t, rows, :] = flow
-        TM[t, rows, :] = turns
-        TN[t, rows, :] = level
-
+    zero = jnp.zeros((DIRS, LANES), F32)
     for t in range(TILES):
-        lanes = slice(t * LANES, (t + 1) * LANES)
-        code = (cg[:, lanes] + 8 * turn[:, lanes] + 64 * sea[:, lanes]).astype(F32)
-        levels(t, slice(0, ROWS), code)
+        for i in (ROWS, RING - 1):
+            Q0[t + 1, pl.ds(i, DIRS, stride=RING), :] = zero
+            Q1[t + 1, pl.ds(i, DIRS, stride=RING), :] = zero
 
     def clear(d, carry):
         rows = pl.ds(pl.multiple_of(d * RING, 8), RING)
@@ -200,8 +136,26 @@
 
     lax.fori_loop(0, DIRS, clear, 0)
 
+    for d in range(DIRS):
+        ay = along[1, d]
+        north = ay * (0.5 + 0.5 * sign[1, d].astype(F32))
+        NO[d : d + 1, :] = jnp.full((1, LANES), north, F32)
+        SO[d : d + 1, :] = jnp.full((1, LANES), ay - north, F32)
+
+    for copy in maps:
+        copy.wait()
+    for t in range(TILES):
+        lanes = slice(t * LANES, (t + 1) * LANES)
+        level = turn[:, lanes].astype(F32)
+        mask = sea[:, lanes].astype(F32)
+        MK[t] = mask
+        CM[t] = (0.1 + 0.8 * cg[:, lanes].astype(F32) / 7.0) * mask
+        TM[t] = (0.3 * jnp.abs(level - 3.5) / 3.5) * mask
+        TN[t] = level
+
     def weigh(t, carry):
-        flow = CM[t, 0:ROWS, :]
+        load(t).wait()
+        flow = CM[t]
 
         def one(d, carry):
             rows = pl.ds(pl.multiple_of(d * RING, 8), ROWS)
@@ -210,22 +164,32 @@
 
         return lax.fori_loop(0, DIRS, one, carry, unroll=4)
 
-    lax.fori_loop(0, TILES, weigh, 0)
-
-    for side, there in ((0, has_prev), (1, has_next)):
-
-        @pl.when(there)
-        def _(side=side):
-            meta_arrived(side).wait_recv()
-
-    for t in range(TILES):
-        lanes = slice(t * LANES, (t + 1) * LANES)
-        blank = jnp.zeros((4, LANES), F32)
-        code = jnp.concatenate([MR[1, :, lanes], blank, MR[0, :, lanes]], axis=0)
-        levels(t, slice(ROWS, RING), code)
+    def packed(first, second):
+        mixed = jnp.concatenate([first[16:], second[16:]], axis=0)
+        return first[:16].astype(BF16), second[:16].astype(BF16), mixed.astype(BF16)
+
+    def unpacked(parts):
+        parts = [part.astype(F32) for part in parts]
+        return [
+            jnp.concatenate([parts[r], parts[2][8 * r : 8 * r + 8]], axis=0) for r in range(2)
+        ]
+
+    def send_halo(h):
+        for k in range(PER):
+            t = h * PER + k
+            lanes = pl.ds(k * LANES, LANES)
+            for side, row in ((0, 0), (1, ROWS - 1)):
+                rows = pl.ds(row, DIRS, stride=RING)
+                for part, value in enumerate(packed(Q0[t + 1, rows, :], Q1[t + 1, rows, :])):
+                    HS[h, side, part, :, lanes] = value
+        for side, there in sides:
+
+            @pl.when(there)
+            def _(side=side):
+                halo_copy(h, side).start()
 
     def take_halo(h):
-        for side, there in ((0, has_prev), (1, has_next)):
+        for side, there in sides:
 
             @pl.when(there)
             def _(side=side):
@@ -234,24 +198,15 @@
         for k in range(PER):
             t = h * PER + k
             lanes = pl.ds(k * LANES, LANES)
-            for side, row in ((0, RING - 2), (1, ROWS)):
-                parts = [HR[h, side, part, :, lanes].astype(F32) for part in range(3)]
-                for i in range(2):
-                    value = jnp.concatenate([parts[i], parts[2][8 * i : 8 * i + 8]], axis=0)
-                    C[t, pl.ds(row + i, DIRS, stride=RING), :] = value
-            zero = jnp.zeros((DIRS, LANES), F32)
-            for i in range(ROWS + 2, RING - 2):
-                C[t, pl.ds(i, DIRS, stride=RING), :] = zero
-            flow = CM[t, ROWS:RING, :]
-
-            def one(d, carry):
-                rows = pl.ds(pl.multiple_of(d * RING + ROWS, 8), RING - ROWS)
-                Q0[t + 1, rows, :] = flow * C[t, rows, :]
-                return carry
-
-            lax.fori_loop(0, DIRS, one, 0, unroll=4)
-
-    lane = iota((RING, LANES), 1)
+            for side, row, beyond, weight in ((0, 0, RING - 1, SO), (1, ROWS - 1, ROWS, NO)):
+                before, after = unpacked([HR[h, side, part, :, lanes] for part in range(3)])
+                rows = pl.ds(row, DIRS, stride=RING)
+                inflow = weight[...] * before
+                D[t, rows, :] = D[t, rows, :] + inflow
+                Q1[t + 1, rows, :] = Q1[t + 1, rows, :] + CM[t, row : row + 1, :] * inflow
+                Q1[t + 1, pl.ds(beyond, DIRS, stride=RING), :] = after
+
+    lane = iota((ROWS, LANES), 1)
 
     def step(t, state, q, result, next_q):
         flow = CM[t]
@@ -260,21 +215,23 @@
         up = TN[t] >= 4.0
 
         def one(d, carry):
-            rows = pl.ds(pl.multiple_of(d * RING, 8), RING)
-            above = pl.ds(pl.multiple_of(lax.rem(d + 1, DIRS) * RING, 8), RING)
-            below = pl.ds(pl.multiple_of(lax.rem(d + DIRS - 1, DIRS) * RING, 8), RING)
+            ring = pl.ds(pl.multiple_of(d * RING, 8), RING)
+            rows = pl.ds(pl.multiple_of(d * RING, 8), ROWS)
+            above = pl.ds(pl.multiple_of(lax.rem(d + 1, DIRS) * RING, 8), ROWS)
+            below = pl.ds(pl.multiple_of(lax.rem(d + DIRS - 1, DIRS) * RING, 8), ROWS)
             ax, ay = along[0, d], along[1, d]
             toward = sign[0, d]
             north = ay * (0.5 + 0.5 * sign[1, d].astype(F32))
             south = ay - north
             c = state[t, rows, :]
-            here = q[t + 1, rows, :]
+            around = q[t + 1, ring, :]
+            here = around[:ROWS]
             edge = jnp.where(toward > 0, 0, LANES - 1)
             shift = jnp.where(toward > 0, LANES - 1, 1)
             beside = q[t + 1 + toward, rows, :]
             from_side = pltpu.roll(jnp.where(lane == edge, beside, here), shift, 1)
-            from_north = pltpu.roll(here, RING - 1, 0)
-            from_south = pltpu.roll(here, 1, 0)
+            from_north = pltpu.roll(around, RING - 1, 0)[:ROWS]
+            from_south = pltpu.roll(around, 1, 0)[:ROWS]
             turned = turns * (jnp.where(up, state[t, above, :], state[t, below, :]) - c)
             new = (
                 mask * c
@@ -283,10 +240,8 @@
                 + (north * from_north + south * from_south)
                 - (ax + ay) * here
             )
-            if next_q is None:
-                result[t, pl.ds(pl.multiple_of(d * RING, 8), ROWS), :] = new[:ROWS]
-            else:
-                result[t, rows, :] = new
+            result[t, rows, :] = new
+            if next_q is not None:
                 next_q[t + 1, rows, :] = flow * new
             return carry
 
@@ -314,35 +269,64 @@
         others = buffer.at[h, :, pl.ds(0, 16 * (n - 1)), :]
         return pltpu.make_async_copy(others, others, sem.at[h])
 
-    def pack_for(h, p, buffer):
-        for k in range(PER):
-            lanes = pl.ds(k * LANES, LANES)
-            for part, value in enumerate(packed(h * PER + k, 2 * p)):
-                buffer[h, part, rows_of(p), lanes] = value
-
+    def dispatch(h, inner, outer):
+        def one(i, carry):
+            p = lax.rem(me + i, n)
+            within = jnp.logical_and(p > 0, p < n - 1)
+
+            def go():
+                for k in range(PER):
+                    t = h * PER + k
+                    lanes = pl.ds(k * LANES, LANES)
+                    first = C[t, pl.ds(2 * p, DIRS, stride=RING), :]
+                    second = C[t, pl.ds(2 * p + 1, DIRS, stride=RING), :]
+                    for part, value in enumerate(packed(first, second)):
+                        S[h, part, rows_of(p), lanes] = value
+
+                @pl.when(i > 0)
+                def _():
+                    exchange(h, p, S, R, s1, r1).start()
+
+            if inner and outer:
+                go()
+            else:
+                pl.when(within if inner else jnp.logical_not(within))(go)
+            return carry
+
+        lax.fori_loop(0, n, one, 0)
+        if outer:
+            R[h, :, rows_of(me), :] = S[h, :, rows_of(me), :]
+
+    lax.fori_loop(0, 2 * PER + 1, weigh, 0)
+    lax.fori_loop(0, 2 * PER, first_step, 0)
+    pl.semaphore_wait(barrier, n - 1 + has_prev.astype(jnp.int32) + has_next.astype(jnp.int32))
+    send_halo(0)
+    send_halo(1)
+    lax.fori_loop(0, PER, second_step, 0)
+    dispatch(0, True, False)
+    lax.fori_loop(2 * PER + 1, TILES, weigh, 0)
+
+    def rest(h, carry):
+        lax.fori_loop(h * PER, h * PER + PER, first_step, 0)
+        send_halo(h)
+        return carry
+
+    lax.fori_loop(2, CHUNKS, rest, 0)
     take_halo(0)
+    take_halo(1)
+    lax.fori_loop(0, PER, second_step, 0)
+    dispatch(0, False, True)
 
     def propagate(h, carry):
         @pl.when(h < CHUNKS - 1)
         def _():
             take_halo(h + 1)
 
-        first = jnp.where(h == 0, 0, h * PER + 1)
-        lax.fori_loop(first, jnp.minimum(h * PER + PER + 1, TILES), first_step, 0)
         lax.fori_loop(h * PER, h * PER + PER, second_step, 0)
-
-        def send(i, carry):
-            p = lax.rem(me + i, n)
-            pack_for(h, p, S)
-            exchange(h, p, S, R, s1, r1).start()
-            return carry
-
-        lax.fori_loop(1, n, send, 0)
-        pack_for(h, me, R)
-        return carry
-
-    lax.fori_loop(0, CHUNKS, propagate, 0)
-
+        dispatch(h, True, True)
+        return carry
+
+    lax.fori_loop(1, CHUNKS, propagate, 0)
     for copy in weights:
         copy.wait()
     wide = (COMPS, 2 * COMPS)
@@ -441,41 +425,44 @@
     for h in range(CHUNKS):
         wgrad[:, h * WIDE : (h + 1) * WIDE] = WG[h]
 
-    def store(t):
-        return pltpu.make_async_copy(
-            C4.at[t, :, pl.ds(0, ROWS), :], out.at[:, :, pl.ds(t * LANES, LANES)], out_sem.at[t]
-        )
-
-    for h in range(CHUNKS):
+    def collect(h, carry):
         all_of(h, IR, r2).wait()
 
         def add(p, carry):
             for k in range(PER):
+                t = h * PER + k
                 lanes = pl.ds(k * LANES, LANES)
-                parts = [IR[h, part, rows_of(p), lanes].astype(F32) for part in range(3)]
+                values = unpacked([IR[h, part, rows_of(p), lanes] for part in range(3)])
                 for r in range(2):
-                    value = jnp.concatenate([parts[r], parts[2][8 * r : 8 * r + 8]], axis=0)
                     rows = pl.ds(2 * p + r, DIRS, stride=RING)
-                    C[h * PER + k, rows, :] = C[h * PER + k, rows, :] + value
+                    D[t, rows, :] = C[t, rows, :] + values[r]
             return carry
 
-        lax.fori_loop(0, n, add, 0)
-        for k in range(PER):
-            store(h * PER + k).start()
-
-    for t in range(TILES):
-        store(t).wait()
-
+        return lax.fori_loop(0, n, add, carry, unroll=2)
+
+    lax.fori_loop(0, CHUNKS, collect, 0)
     for h in range(CHUNKS):
         all_of(h, S, s1).wait()
         all_of(h, IS, s2).wait()
-    for side, there in ((0, has_prev), (1, has_next)):
+    for side, there in sides:
 
         @pl.when(there)
         def _(side=side):
-            meta_copies(side).wait_send()
             for h in range(CHUNKS):
-                halo_copies(h, side).wait_send()
+                halo_copy(h, side).wait_send()
+
+
+def finish(total, slope, out, wgrad, out_sem, w_sem):
+    def store(t):
+        return pltpu.make_async_copy(
+            total.at[t, :, pl.ds(0, ROWS), :], out.at[:, :, pl.ds(t * LANES, LANES)], out_sem.at[t]
+        )
+
+    copies = [store(t) for t in range(TILES)] + [pltpu.make_async_copy(slope, wgrad, w_sem)]
+    for copy in copies:
+        copy.start()
+    for copy in copies:
+        copy.wait()
 
 
 def shards(n, slabs, forcing, state, wind, cg, turn, sea, sign, w_in, w_out, ww):
@@ -489,18 +476,17 @@
     sems = pltpu.SemaphoreType.DMA
     field = (TILES, DIRS, RING, LANES)
     fluxes = (TILES + 2, DIRS * RING, LANES)
-    cells = (TILES, RING, LANES)
+    cells = (TILES, ROWS, LANES)
     message = (CHUNKS, 3, 16 * n, WIDE)
-    return pl.pallas_call(
+    total, slope = pl.pallas_call(
         functools.partial(kernel, n, slabs),
         out_shape=(
-            jax.ShapeDtypeStruct(forcing.shape, F32),
-            jax.ShapeDtypeStruct(wind.shape, F32),
+            pltpu.VMEM(field, F32),
+            pltpu.VMEM(wind.shape, F32),
         ),
         in_specs=[hbm] * 9 + [smem] * 2,
-        out_specs=(hbm, vmem),
+        out_specs=(vmem, vmem),
         scratch_shapes=[
-            pltpu.VMEM(field, F32),
             pltpu.VMEM(field, F32),
             pltpu.VMEM(fluxes, F32),
             pltpu.VMEM(fluxes, F32),
@@ -508,10 +494,10 @@
             pltpu.VMEM(cells, F32),
             pltpu.VMEM(cells, F32),
             pltpu.VMEM(cells, F32),
+            pltpu.VMEM((DIRS, LANES), F32),
+            pltpu.VMEM((DIRS, LANES), F32),
             pltpu.VMEM((CHUNKS, 2, 3, 16, WIDE), BF16),
             pltpu.VMEM((CHUNKS, 2, 3, 16, WIDE), BF16),
-            pltpu.VMEM((2, 2, TILES * LANES), F32),
-            pltpu.VMEM((2, 2, TILES * LANES), F32),
             pltpu.VMEM(message, BF16),
             pltpu.VMEM(message, BF16),
             pltpu.VMEM(message, BF16),
@@ -535,19 +521,28 @@
             sems((7 + CHUNKS,)),
             sems((CHUNKS, 2)),
             sems((CHUNKS, 2)),
-            sems((2,)),
-            sems((2,)),
             sems((CHUNKS,)),
             sems((CHUNKS,)),
             sems((CHUNKS,)),
             sems((CHUNKS,)),
-            sems((TILES,)),
         ],
         compiler_params=pltpu.CompilerParams(
             collective_id=0, has_side_effects=True, vmem_limit_bytes=58 << 20
         ),
         name="adjoint_window",
     )(forcing, state, w_in, w_out, cg, turn, sea, wind, ww, sign, along)
+    return pl.pallas_call(
+        finish,
+        out_shape=(
+            jax.ShapeDtypeStruct(forcing.shape, F32),
+            jax.ShapeDtypeStruct(wind.shape, F32),
+        ),
+        in_specs=[vmem] * 2,
+        out_specs=(hbm, hbm),
+        scratch_shapes=[sems((TILES,)), sems],
+        compiler_params=pltpu.CompilerParams(vmem_limit_bytes=16 << 20),
+        name="finish",
+    )(total, slope)
 
 
 def solution(mesh):

time: 59.2 us -> 55 us (0.929); the launches traced: 59 us -> 54.2 us
  local copies, waits for them, and re-layouts: 4.58 us -> 0 us
    unnamed x4 -> x0, local copies, waits for them, and re-layouts: 4.58 us -> none
    pallas_call x1 -> x2, Pallas kernels: 53.8 us -> 53.5 us  [the longest x1 51.8 us: shards(): pl.pallas_call(functools.partial(kernel, n, slabs), out_shape=(pltpu.VMEM...]
where the time goes in v3:
time: 55 us; the launch traced here: 54.2 us
  Pallas kernels  53.5 us (97%)
  between operations  0.64 us (1%)
    pallas_call x1, Pallas kernels, shards(): pl.pallas_call(functools.partial(kernel, n, slabs), out_shape=(pltpu.VMEM...  51.8 us
    pallas_call x1, Pallas kernels, shards(): pl.pallas_call(finish, out_shape=(jax.ShapeDtypeStruct(forcing.shape, F32...  1.73 us

profile of v3, /device:TPU:7, one launch (start us, length us, event | category | flops | bytes accessed | tf_op | source)
XLA Modules:
  0.0 54.2 jit_solution(3401129906689408126)
XLA Ops:
  0.6 51.8 %adjoint_window.1 = (f32[8,24,40,128]{3,2,1,0:T(8,128)S(1)}, f32[2,1024]{1,0:T(2,128)S(1)}) custom-call(f32[24,32,1024]{2,1,0:T(8,128)} %forcing.1, bf16[384,2,1024]{2,1,0:T(2,128)(2,1)} %fs.1, bf16[1536,384]{1,0:T(8,128)(2,1)} %w_in_hbm.1, bf16[384,1536]{1,0:T(8,128)(2,1)} %w_out_hbm.1, s32[1,32,1024]{2,1,0:T(8,128)} %cg_hbm.1, s32[1,32,1024]{2,1,0:T(8,128)} %turn_hbm.1, ...), custom_call_target="tpu_custom_call" | custom-call | tf_op jit(solution)/shard_map/adjoint_window/pallas_call | solution.py:481
  52.4 1.7 %finish.1 = (f32[24,32,1024]{2,1,0:T(8,128)}, f32[2,1024]{1,0:T(2,128)}) custom-call(f32[8,24,40,128]{3,2,1,0:T(8,128)S(1)} %get-tuple-element.4.total, f32[2,1024]{1,0:T(2,128)S(1)} %get-tuple-element.5.slope), custom_call_target="tpu_custom_call" | custom-call | tf_op jit(solution)/shard_map/finish/pallas_call | solution.py:534

commit v4 on v3

--- a/solution.py
+++ b/solution.py
@@ -17,6 +17,7 @@
 TILES = 8
 CHUNKS = 4
 PER = TILES // CHUNKS
+EARLY = 2
 WIDE = PER * LANES
 HID = 1536
 BLOCK = 256
@@ -44,6 +45,20 @@
 ):
     me = lax.axis_index("comp")
     slab = lax.axis_index("space")
+
+    barrier = pltpu.get_barrier_semaphore()
+    has_prev = slab > 0
+    has_next = slab < slabs - 1
+    sides = ((0, has_prev), (1, has_next))
+
+    @pl.when(has_prev)
+    def _():
+        pl.semaphore_signal(barrier, inc=1, device_id={"space": slab - 1}, device_id_type=MESH)
+
+    @pl.when(has_next)
+    def _():
+        pl.semaphore_signal(barrier, inc=1, device_id={"space": slab + 1}, device_id_type=MESH)
+
     C = C4.reshape(TILES, DIRS * RING, LANES)
     D = D4.reshape(TILES, DIRS * RING, LANES)
 
@@ -74,8 +89,6 @@
         for h in range(CHUNKS)
     ]
 
-    barrier = pltpu.get_barrier_semaphore()
-
     def greet(step, carry):
         pl.semaphore_signal(
             barrier, inc=1, device_id={"comp": lax.rem(me + step, n)}, device_id_type=MESH
@@ -83,17 +96,6 @@
         return carry
 
     lax.fori_loop(1, n, greet, 0)
-    has_prev = slab > 0
-    has_next = slab < slabs - 1
-    sides = ((0, has_prev), (1, has_next))
-
-    @pl.when(has_prev)
-    def _():
-        pl.semaphore_signal(barrier, inc=1, device_id={"space": slab - 1}, device_id_type=MESH)
-
-    @pl.when(has_next)
-    def _():
-        pl.semaphore_signal(barrier, inc=1, device_id={"space": slab + 1}, device_id_type=MESH)
 
     for copy in weights:
         copy.start()
@@ -174,7 +176,7 @@
             jnp.concatenate([parts[r], parts[2][8 * r : 8 * r + 8]], axis=0) for r in range(2)
         ]
 
-    def send_halo(h):
+    def pack_halo(h):
         for k in range(PER):
             t = h * PER + k
             lanes = pl.ds(k * LANES, LANES)
@@ -182,6 +184,8 @@
                 rows = pl.ds(row, DIRS, stride=RING)
                 for part, value in enumerate(packed(Q0[t + 1, rows, :], Q1[t + 1, rows, :])):
                     HS[h, side, part, :, lanes] = value
+
+    def send_halo(h):
         for side, there in sides:
 
             @pl.when(there)
@@ -297,36 +301,46 @@
         if outer:
             R[h, :, rows_of(me), :] = S[h, :, rows_of(me), :]
 
-    lax.fori_loop(0, 2 * PER + 1, weigh, 0)
-    lax.fori_loop(0, 2 * PER, first_step, 0)
+    lax.fori_loop(0, TILES, weigh, 0)
+    lax.fori_loop(0, TILES, first_step, 0)
+
+    def pack_all(h, carry):
+        pack_halo(h)
+        return carry
+
+    lax.fori_loop(0, CHUNKS, pack_all, 0)
     pl.semaphore_wait(barrier, n - 1 + has_prev.astype(jnp.int32) + has_next.astype(jnp.int32))
-    send_halo(0)
-    send_halo(1)
-    lax.fori_loop(0, PER, second_step, 0)
-    dispatch(0, True, False)
-    lax.fori_loop(2 * PER + 1, TILES, weigh, 0)
-
-    def rest(h, carry):
-        lax.fori_loop(h * PER, h * PER + PER, first_step, 0)
+    for h in range(CHUNKS):
         send_halo(h)
-        return carry
-
-    lax.fori_loop(2, CHUNKS, rest, 0)
-    take_halo(0)
-    take_halo(1)
-    lax.fori_loop(0, PER, second_step, 0)
-    dispatch(0, False, True)
-
-    def propagate(h, carry):
-        @pl.when(h < CHUNKS - 1)
+
+    def ahead(h, carry):
+        lax.fori_loop(h * PER, h * PER + PER, second_step, 0)
+        dispatch(h, True, False)
+        return carry
+
+    lax.fori_loop(0, EARLY, ahead, 0)
+
+    def behind(h, carry):
+        take_halo(h)
+
+        @pl.when(h > 0)
         def _():
-            take_halo(h + 1)
-
-        lax.fori_loop(h * PER, h * PER + PER, second_step, 0)
-        dispatch(h, True, True)
-        return carry
-
-    lax.fori_loop(1, CHUNKS, propagate, 0)
+            lax.fori_loop((h - 1) * PER, h * PER, second_step, 0)
+
+            @pl.when(h <= EARLY)
+            def _():
+                dispatch(h - 1, False, True)
+
+            @pl.when(h > EARLY)
+            def _():
+                dispatch(h - 1, True, True)
+
+        return carry
+
+    lax.fori_loop(0, CHUNKS, behind, 0)
+    lax.fori_loop(TILES - PER, TILES, second_step, 0)
+    dispatch(CHUNKS - 1, True, True)
+
     for copy in weights:
         copy.wait()
     wide = (COMPS, 2 * COMPS)
@@ -438,7 +452,7 @@
                     D[t, rows, :] = C[t, rows, :] + values[r]
             return carry
 
-        return lax.fori_loop(0, n, add, carry, unroll=2)
+        return lax.fori_loop(0, n, add, carry, unroll=4)
 
     lax.fori_loop(0, CHUNKS, collect, 0)
     for h in range(CHUNKS):

time: 55 us -> 52.9 us (0.962)
  Pallas kernels: 53.5 us -> 51.5 us
    pallas_call x1, Pallas kernels: 51.8 us -> 49.8 us  [shards(): pl.pallas_call(functools.partial(kernel, n, slabs), out_shape=(pltpu.VMEM...]
where the time goes in v4:
time: 52.9 us; the launch traced here: 52.2 us
  Pallas kernels  51.5 us (97%)
  between operations  0.64 us (1%)
    pallas_call x1, Pallas kernels, shards(): pl.pallas_call(functools.partial(kernel, n, slabs), out_shape=(pltpu.VMEM...  49.8 us
    pallas_call x1, Pallas kernels, shards(): pl.pallas_call(finish, out_shape=(jax.ShapeDtypeStruct(forcing.shape, F32...  1.73 us

profile of v4, /device:TPU:7, one launch (start us, length us, event | category | flops | bytes accessed | tf_op | source)
XLA Modules:
  0.0 52.2 jit_solution(10639108822589254782)
XLA Ops:
  0.6 49.8 %adjoint_window.1 = (f32[8,24,40,128]{3,2,1,0:T(8,128)S(1)}, f32[2,1024]{1,0:T(2,128)S(1)}) custom-call(f32[24,32,1024]{2,1,0:T(8,128)} %forcing.1, bf16[384,2,1024]{2,1,0:T(2,128)(2,1)} %fs.1, bf16[1536,384]{1,0:T(8,128)(2,1)} %w_in_hbm.1, bf16[384,1536]{1,0:T(8,128)(2,1)} %w_out_hbm.1, s32[1,32,1024]{2,1,0:T(8,128)} %cg_hbm.1, s32[1,32,1024]{2,1,0:T(8,128)} %turn_hbm.1, ...), custom_call_target="tpu_custom_call" | custom-call | tf_op jit(solution)/shard_map/adjoint_window/pallas_call | solution.py:495
  50.4 1.7 %finish.1 = (f32[24,32,1024]{2,1,0:T(8,128)}, f32[2,1024]{1,0:T(2,128)}) custom-call(f32[8,24,40,128]{3,2,1,0:T(8,128)S(1)} %get-tuple-element.4.total, f32[2,1024]{1,0:T(2,128)S(1)} %get-tuple-element.5.slope), custom_call_target="tpu_custom_call" | custom-call | tf_op jit(solution)/shard_map/finish/pallas_call | solution.py:548

commit v5 on v4

--- a/solution.py
+++ b/solution.py
@@ -17,7 +17,7 @@
 TILES = 8
 CHUNKS = 4
 PER = TILES // CHUNKS
-EARLY = 2
+EARLY = 3
 WIDE = PER * LANES
 HID = 1536
 BLOCK = 256

time: 52.9 us -> 51.8 us (0.979)
  Pallas kernels: 51.5 us -> 50.6 us
    pallas_call x1, Pallas kernels: 49.8 us -> 48.8 us  [shards(): pl.pallas_call(functools.partial(kernel, n, slabs), out_shape=(pltpu.VMEM...]
where the time goes in v5:
time: 51.8 us; the launch traced here: 51.2 us
  Pallas kernels  50.6 us (98%)
  between operations  0.64 us (1%)
    pallas_call x1, Pallas kernels, shards(): pl.pallas_call(functools.partial(kernel, n, slabs), out_shape=(pltpu.VMEM...  48.8 us
    pallas_call x1, Pallas kernels, shards(): pl.pallas_call(finish, out_shape=(jax.ShapeDtypeStruct(forcing.shape, F32...  1.73 us

profile of v5, /device:TPU:7, one launch (start us, length us, event | category | flops | bytes accessed | tf_op | source)
XLA Modules:
  0.0 51.2 jit_solution(7205745005692051912)
XLA Ops:
  0.6 48.8 %adjoint_window.1 = (f32[8,24,40,128]{3,2,1,0:T(8,128)S(1)}, f32[2,1024]{1,0:T(2,128)S(1)}) custom-call(f32[24,32,1024]{2,1,0:T(8,128)} %forcing.1, bf16[384,2,1024]{2,1,0:T(2,128)(2,1)} %fs.1, bf16[1536,384]{1,0:T(8,128)(2,1)} %w_in_hbm.1, bf16[384,1536]{1,0:T(8,128)(2,1)} %w_out_hbm.1, s32[1,32,1024]{2,1,0:T(8,128)} %cg_hbm.1, s32[1,32,1024]{2,1,0:T(8,128)} %turn_hbm.1, ...), custom_call_target="tpu_custom_call" | custom-call | tf_op jit(solution)/shard_map/adjoint_window/pallas_call | solution.py:495
  49.5 1.7 %finish.1 = (f32[24,32,1024]{2,1,0:T(8,128)}, f32[2,1024]{1,0:T(2,128)}) custom-call(f32[8,24,40,128]{3,2,1,0:T(8,128)S(1)} %get-tuple-element.4.total, f32[2,1024]{1,0:T(2,128)S(1)} %get-tuple-element.5.slope), custom_call_target="tpu_custom_call" | custom-call | tf_op jit(solution)/shard_map/finish/pallas_call | solution.py:548

commit v6 on v5

--- a/solution.py
+++ b/solution.py
@@ -58,6 +58,14 @@
     @pl.when(has_next)
     def _():
         pl.semaphore_signal(barrier, inc=1, device_id={"space": slab + 1}, device_id_type=MESH)
+
+    def greet(step, carry):
+        pl.semaphore_signal(
+            barrier, inc=1, device_id={"comp": lax.rem(me + step, n)}, device_id_type=MESH
+        )
+        return carry
+
+    lax.fori_loop(1, n, greet, 0)
 
     C = C4.reshape(TILES, DIRS * RING, LANES)
     D = D4.reshape(TILES, DIRS * RING, LANES)
@@ -88,14 +96,6 @@
         )
         for h in range(CHUNKS)
     ]
-
-    def greet(step, carry):
-        pl.semaphore_signal(
-            barrier, inc=1, device_id={"comp": lax.rem(me + step, n)}, device_id_type=MESH
-        )
-        return carry
-
-    lax.fori_loop(1, n, greet, 0)
 
     for copy in weights:
         copy.start()

time: 51.8 us -> 52.1 us (level)
  Pallas kernels: 50.6 us -> 51.3 us
    pallas_call x1, Pallas kernels: 48.8 us -> 49.6 us  [shards(): pl.pallas_call(functools.partial(kernel, n, slabs), out_shape=(pltpu.VMEM...]
where the time goes in v6:
time: 52.1 us; the launch traced here: 52 us
  Pallas kernels  51.3 us (98%)
  between operations  0.64 us (1%)
    pallas_call x1, Pallas kernels, shards(): pl.pallas_call(functools.partial(kernel, n, slabs), out_shape=(pltpu.VMEM...  49.6 us
    pallas_call x1, Pallas kernels, shards(): pl.pallas_call(finish, out_shape=(jax.ShapeDtypeStruct(forcing.shape, F32...  1.73 us

profile of v6, /device:TPU:7, one launch (start us, length us, event | category | flops | bytes accessed | tf_op | source)
XLA Modules:
  0.0 52.0 jit_solution(407198297533601920)
XLA Ops:
  0.6 49.6 %adjoint_window.1 = (f32[8,24,40,128]{3,2,1,0:T(8,128)S(1)}, f32[2,1024]{1,0:T(2,128)S(1)}) custom-call(f32[24,32,1024]{2,1,0:T(8,128)} %forcing.1, bf16[384,2,1024]{2,1,0:T(2,128)(2,1)} %fs.1, bf16[1536,384]{1,0:T(8,128)(2,1)} %w_in_hbm.1, bf16[384,1536]{1,0:T(8,128)(2,1)} %w_out_hbm.1, s32[1,32,1024]{2,1,0:T(8,128)} %cg_hbm.1, s32[1,32,1024]{2,1,0:T(8,128)} %turn_hbm.1, ...), custom_call_target="tpu_custom_call" | custom-call | tf_op jit(solution)/shard_map/adjoint_window/pallas_call | solution.py:495
  50.2 1.7 %finish.1 = (f32[24,32,1024]{2,1,0:T(8,128)}, f32[2,1024]{1,0:T(2,128)}) custom-call(f32[8,24,40,128]{3,2,1,0:T(8,128)S(1)} %get-tuple-element.4.total, f32[2,1024]{1,0:T(2,128)S(1)} %get-tuple-element.5.slope), custom_call_target="tpu_custom_call" | custom-call | tf_op jit(solution)/shard_map/finish/pallas_call | solution.py:548
